TPU v7x, 128 devices: a whole 4x4x4 slice. The times are simulated.
128 devices in a mesh: band: 4 (over z_lo, core), space: 32 (over x, y, z_hi).
Axes of the slice: x: 4, y: 4, z: 4 (z_hi: 2, z_lo: 2; z = z_hi * 2 + z_lo), core: 2. Of those that a mesh axis runs over, the one named last changes fastest.
Arguments:
- orbitals: float32 [16, 384, 32, 128], P('band', 'space'), may hold values from -8.5 to 8.5
- potential: float32 [384, 32, 128], P('space'), may hold values from 0 to 0.6
- rotation: float32 [16, 16], replicated, may hold values from -1.5 to 1.5
Outputs:
- rotated: float32 [16, 384, 32, 128], P('band', 'space')
All inputs are finite; a program needn't handle non-finite values.
Results may differ from a plain program's by a relative error of at most 0.00024.
Values sent between devices are 32-bit elements; how exact they have to be, the bound alone decides.
No kernel may reach another device: no remote copies, remote signals or barrier semaphores. Data moves between devices by JAX's collectives and lax.ppermute only.
A program may use at most 192 MiB of HBM per device.

v0:
```python
import jax
import jax.numpy as jnp
import ml_dtypes
import numpy as np
from jax import lax
from jax.experimental import pallas as pl
from jax.experimental.pallas import tpu as pltpu
from jax.sharding import PartitionSpec as P


NY, NZ = 32, 128
DEGREE = 8
RADIUS = 6
SLAB = 12
RUN = 3
SEG = 48
COEFS = (
    -5369.0 / 1800.0,
    12.0 / 7.0,
    -15.0 / 56.0,
    10.0 / 189.0,
    -1.0 / 112.0,
    2.0 / 1925.0,
    -1.0 / 16632.0,
)
CENTER = 6.75
HALF_WIDTH = 6.25
GAINS = tuple(-c / HALF_WIDTH for c in COEFS)
POT_SCALE = 2.0 / HALF_WIDTH
BF16, F32 = jnp.bfloat16, jnp.float32
AXES = ("band", "space")
VMEM_LIMIT = 48 * 1024 * 1024


def split_gain(j):
    high = np.float32(GAINS[j]).astype(ml_dtypes.bfloat16)
    low = np.float32(GAINS[j] - float(high)).astype(ml_dtypes.bfloat16)
    return high, low


def circulant(n):
    high = np.zeros((n, n), ml_dtypes.bfloat16)
    low = np.zeros((n, n), ml_dtypes.bfloat16)
    for j in range(1, RADIUS + 1):
        for i in range(n):
            for k in ((i + j) % n, (i - j) % n):
                high[i, k], low[i, k] = split_gain(j)
    return high, low


GAIN_GAP = 4.0 * sum(
    GAINS[j] - float(split_gain(j)[0]) - float(split_gain(j)[1]) for j in range(1, RADIUS + 1)
)
POT_SHIFT = (-2.0 * CENTER - 3.0 * COEFS[0]) / HALF_WIDTH + GAIN_GAP


def z_matrix():
    high, low = circulant(NZ)
    return np.block([[high, low], [high, np.zeros_like(low)]])


def y_matrix():
    high, low = circulant(NY)
    return np.concatenate([high, high, low], axis=1)


def index_of(x, y, z, core):
    return ((z % 2) * 2 + core) * 32 + (x % 4) * 8 + y * 2 + z // 2


DEVICES = [(x, y, z, c) for x in range(4) for y in range(4) for z in range(4) for c in range(2)]


def permute(array, target):
    pairs = []
    for device in DEVICES:
        to = target(*device)
        if to is not None:
            pairs.append((index_of(*device), index_of(*to)))
    return lax.ppermute(array, AXES, pairs)


def other_core(x, y, z, core):
    return (x, y, z, 1 - core)


def x_neighbour(x, y, z, core):
    return (x - 1, y, z, 1) if core == 0 else (x + 1, y, z, 0)


def host_of(c):
    lo, core, i = c >> 3, (c >> 2) & 1, c & 3
    return core * 2 + (i >> 1), 2 * (i & 1) + 1 - lo


HOSTS = [host_of(c) for c in range(16)]


def low_slab(y, core):
    return (y // 2) ^ (y % 2) ^ core


def source_of_run(core):
    runs = [low_slab(y, core) * 8 + (z // 2) * 4 + (y // 2) * 2 + z % 2 for y, z in HOSTS]
    return [runs.index(run) for run in range(16)]


def place():
    band, space = lax.axis_index("band"), lax.axis_index("space")
    return band // 2, band % 2, (space // 2) % 4, space % 2


def mix_kernel(rotation, first, second, third, fourth, out):
    lo, core, y, hi = place()
    mine = (y // 2) * 2 + lo
    for c in range(0, 16, 2):
        totals = [None, None]
        for r, ref in enumerate((first, second, third, fourth)):
            for i in range(4):
                cells = ref[i]
                for d in range(2):
                    term = rotation[4 * (r ^ mine) + i, c + d] * cells
                    totals[d] = term if totals[d] is None else totals[d] + term
        for d in range(2):
            out[c + d] = totals[d]


def block(a, b, w, w_at, zmat, ymat, at, first):
    n = SLAB
    u = a[at : at + n]
    high = u.astype(BF16)
    low = (u - high.astype(F32)).astype(BF16)
    both = jnp.concatenate([high.reshape(n * NY, NZ), low.reshape(n * NY, NZ)], axis=1)
    zz = jnp.dot(both, zmat[...], preferred_element_type=F32)
    z = (zz[:, :NZ] + zz[:, NZ:]).reshape(n, NY, NZ)
    ys = []
    for i in range(0, n, 2):
        rows = [jnp.concatenate([q[i], q[i + 1]], axis=1) for q in (high, low, high)]
        pair = jnp.dot(ymat[...], jnp.concatenate(rows, axis=0), preferred_element_type=F32)
        ys += [pair[:, :NZ], pair[:, NZ:]]
    for r in range(0, NY, 8):
        x = a[at - RADIUS : at + n + RADIUS, r : r + 8]
        total = w[at - w_at : at - w_at + n, r : r + 8] * x[RADIUS : RADIUS + n] + z[:, r : r + 8]
        total = total + jnp.stack([t[r : r + 8] for t in ys])
        for j in range(1, RADIUS + 1):
            near = x[RADIUS + j : RADIUS + j + n] + x[RADIUS - j : RADIUS - j + n]
            total = total + GAINS[j] * near
        if first:
            b[at : at + n, r : r + 8] = 0.5 * total
        else:
            b[at : at + n, r : r + 8] = total - b[at : at + n, r : r + 8]


KEPT = SEG - RADIUS


def lay_segment(ref, to, at, core, same):
    ahead = source_of_run(1 if same else 0)
    back = source_of_run(0 if same else 1)
    for s in range(16):
        source = jnp.where(core == 1, ahead[s], back[15 - s])
        for t in range(RUN):
            to[at + RUN * s + t] = ref[source, jnp.where(core == 1, t, RUN - 1 - t)]


def lay_potential(ref, to, at, core, core_from, y, hi):
    for s in range(4):
        slab = jnp.where(core == 1, s, 3 - s)
        source = ((slab & 1) ^ hi) * 2 + ((slab >> 1) ^ low_slab(y, core_from))
        for t in range(SLAB):
            plane = ref[source, jnp.where(core == 1, t, SLAB - 1 - t)]
            to[at + SLAB * s + t] = plane * POT_SCALE + POT_SHIFT


def first_kernel(own, other, pot, pot_other, zmat, ymat, even_out, odd_out, w_out, even, odd, w):
    lo, core, y, hi = place()
    lay_segment(other, even, 0, core, False)
    lay_segment(own, even, SEG, core, True)
    lay_potential(pot_other, w, 0, core, 1 - core, y, hi)
    lay_potential(pot, w, SEG, core, core, y, hi)
    for k in range(1, DEGREE):
        a, b = (even, odd) if k % 2 else (odd, even)
        for at in range(RADIUS * k, 2 * SEG - RADIUS * k, SLAB):
            block(a, b, w, 0, zmat, ymat, at, k == 1)
    even_out[...] = even[KEPT:]
    odd_out[...] = odd[KEPT:]
    w_out[...] = w[SEG:]


def second_kernel(even_in, odd_in, w_in, halo, pot, zmat, ymat, out, even, odd, w):
    lo, core, y, hi = place()
    shift = KEPT
    even[0 : 2 * SEG - shift] = even_in[...]
    odd[0 : 2 * SEG - shift] = odd_in[...]
    w[0:SEG] = w_in[...]
    lay_segment(halo, even, 2 * SEG - shift, core, False)
    lay_potential(pot, w, SEG, core, 1 - core, y, hi)
    for k in range(1, DEGREE + 1):
        a, b = (even, odd) if k % 2 else (odd, even)
        for at in range(2 * SEG - RADIUS * k, 3 * SEG - RADIUS * k, SLAB):
            block(a, b, w, SEG - shift, zmat, ymat, at - shift, k == 1)
    mine = (y % 2) * 2 + hi
    for s in range(4):
        slot = jnp.where(core == 1, s, 3 - s) ^ mine
        for t in range(SLAB):
            plane = even[SEG - shift + SLAB * s + t]
            out[slot, jnp.where(core == 1, t, SLAB - 1 - t)] = plane


def planes(*lead):
    return jax.ShapeDtypeStruct((*lead, NY, NZ), F32)


def vmem(n):
    return [pl.BlockSpec(memory_space=pltpu.VMEM)] * n


def call(kernel, outs, scratch, flops, *operands, scalars=0):
    specs = [pl.BlockSpec(memory_space=pltpu.SMEM)] * scalars + vmem(len(operands) - scalars)
    moved = 4 * sum(x.size for x in (*operands, *outs))
    return pl.pallas_call(
        kernel,
        out_shape=outs,
        in_specs=specs,
        out_specs=vmem(len(outs)),
        scratch_shapes=[pltpu.VMEM((n, NY, NZ), F32) for n in scratch],
        compiler_params=pltpu.CompilerParams(vmem_limit_bytes=VMEM_LIMIT),
        cost_estimate=pl.CostEstimate(flops=flops, bytes_accessed=moved, transcendentals=0),
    )(*operands)


def spread_run(orbitals, band, r):
    def to_run(x, y, z, c):
        run = r ^ (2 * (z % 2) + c)
        far, core = run >> 1, y // 2
        return (x, 2 * far + ((y % 2) ^ core ^ far), 2 * (z // 2) + (run & 1), core)

    return permute(lax.dynamic_slice_in_dim(orbitals, RUN * (r ^ band), RUN, 1), to_run)


def local(orbitals, potential, rotation):
    lo, core, y, hi = place()
    groups = [spread_run(orbitals, 2 * lo + core, r) for r in range(4)]
    near = permute(potential, lambda x, y, z, c: (x, 3 - y, z, c) if c == y // 2 else None)
    near = jnp.where(core == y // 2, potential, near)
    far = permute(potential, lambda x, y, z, c: (x, y ^ 1 if c == y // 2 else y ^ 2, z, y // 2))
    pair = jnp.stack([near, far])
    next_z = permute(pair, lambda x, y, z, c: (x, y, 3 - z, c))
    pot = jnp.concatenate([pair, next_z])
    (mixed,) = call(mix_kernel, [planes(16, RUN)], [], 1 << 22, rotation, *groups, scalars=1)
    pot_halo = permute(pot, x_neighbour)
    pot_other = permute(pot, other_core)
    plane_of_hosts = [[index_of(x, *chip, c) for chip in HOSTS] for x in range(4) for c in range(2)]
    own = lax.all_to_all(mixed, AXES, 0, 0, tiled=True, axis_index_groups=plane_of_hosts)
    own, pot_halo, pot_other = lax.optimization_barrier((own, pot_halo, pot_other))
    other = permute(own, other_core)
    halo = permute(own, x_neighbour)

    zmat, ymat = jnp.asarray(z_matrix()), jnp.asarray(y_matrix())
    kept = 2 * SEG - KEPT
    even, odd, w = call(
        first_kernel,
        [planes(kept), planes(kept), planes(SEG)],
        [2 * SEG, 2 * SEG, 2 * SEG],
        1 << 29,
        own,
        other,
        pot,
        pot_other,
        zmat,
        ymat,
    )
    (filtered,) = call(
        second_kernel,
        [planes(4, SLAB)],
        [3 * SEG - KEPT, 3 * SEG - KEPT, 2 * SEG],
        1 << 29,
        even,
        odd,
        w,
        halo,
        pot_halo,
        zmat,
        ymat,
    )

    result = jnp.zeros(orbitals.shape, F32)
    mine = (y % 2) * 2 + hi
    for r in range(4):

        def to_owner(x, y, z, c):
            slab = r ^ ((y % 2) * 2 + z // 2)
            return (x, 2 * c + (slab >> 1), 2 * (slab & 1) + 1 - z % 2, y // 2)

        piece = permute(filtered[r], to_owner)
        result = lax.dynamic_update_slice_in_dim(result, piece[None], r ^ mine, 0)
    return result


def solution(mesh):
    return jax.shard_map(
        local,
        mesh=mesh,
        in_specs=(P("band", "space", None, None), P("space", None, None), P()),
        out_specs=P("band", "space", None, None),
        check_vma=False,
    )
```

profile of v0, /device:TPU:1, one launch (start us, length us, event | category | flops | bytes accessed | tf_op | source)
XLA Modules:
  0.0 87.3 jit_solution(15371311900279675623)
XLA Ops:
  0.0 1.4 %collective-permute-start.4 = (f32[12,32,128]{2,1,0:T(8,128)}, f32[12,32,128]{2,1,0:T(8,128)S(1)}, u32[]{:S(2)}, u32[]{:S(2)}) collective-permute-start(f32[12,32,128]{2,1,0:T(8,128)} %param.6), channel_id=1, source_target_pairs={{0,6},{64,70},{1,7},{65,71},{2,4},{66,68},{3,5},{67,69},{36,34},{1... | collective-permute-start | bytes 589832 | tf_op jit(solution)/shard_map/ppermute | solution.py:80
  1.4 4.4 %collective-permute-start.5 = (f32[12,32,128]{2,1,0:T(8,128)}, f32[12,32,128]{2,1,0:T(8,128)S(1)}, u32[]{:S(2)}, u32[]{:S(2)}) collective-permute-start(f32[12,32,128]{2,1,0:T(8,128)} %param.6), channel_id=1, source_target_pairs={{0,2},{32,4},{64,66},{96,68},{1,3},{33,5},{65,67},{97,69},{2,0},{3... | collective-permute-start | bytes 589832 | tf_op jit(solution)/shard_map/ppermute | solution.py:80
  5.8 3.5 %collective-permute-done.4 = f32[12,32,128]{2,1,0:T(8,128)S(1)} collective-permute-done((f32[12,32,128]{2,1,0:T(8,128)}, f32[12,32,128]{2,1,0:T(8,128)S(1)}, u32[]{:S(2)}, u32[]{:S(2)}) %collective-permute-start.4) | collective-permute-done | bytes 196640 | tf_op jit(solution)/shard_map/ppermute | solution.py:80
  9.4 1.9 %collective-permute-done.5 = f32[12,32,128]{2,1,0:T(8,128)S(1)} collective-permute-done((f32[12,32,128]{2,1,0:T(8,128)}, f32[12,32,128]{2,1,0:T(8,128)S(1)}, u32[]{:S(2)}, u32[]{:S(2)}) %collective-permute-start.5) | collective-permute-done | bytes 196640 | tf_op jit(solution)/shard_map/ppermute | solution.py:80
  11.4 3.5 %collective-permute-start.6 = (f32[2,12,32,128]{3,2,1,0:T(8,128)S(1)}, f32[2,12,32,128]{3,2,1,0:T(8,128)S(1)}, u32[]{:S(2)}, u32[]{:S(2)}) collective-permute-start(f32[2,12,32,128]{3,2,1,0:T(8,128)S(1)} %pad_maximum_fusion.1), channel_id=1, source_target_pairs={{0,65},{32,97},{64,1},{96,33},{1,64},{33,96},{65,0},{97,32},{2,67}... | collective-permute-start | bytes 1179656 | tf_op jit(solution)/shard_map/ppermute | solution.py:80
  14.9 3.2 %collective-permute-start = (f32[4,3,32,128]{3,2,1,0:T(8,128)S(1)}, f32[4,3,32,128]{3,2,1,0:T(8,128)S(1)}, u32[]{:S(2)}, u32[]{:S(2)}) collective-permute-start(f32[4,3,32,128]{3,2,1,0:T(8,128)S(1)} %get-tuple-element.23), channel_id=1, source_target_pairs={{0,0},{32,64},{64,6},{96,70},{1,1},{33,65},{65,7},{97,71},{2,2},{3... | collective-permute-start | bytes 589832 | tf_op jit(solution)/shard_map/ppermute | solution.py:80
  18.1 2.0 %collective-permute-start.2 = (f32[4,3,32,128]{3,2,1,0:T(8,128)S(1)}, f32[4,3,32,128]{3,2,1,0:T(8,128)S(1)}, u32[]{:S(2)}, u32[]{:S(2)}) collective-permute-start(f32[4,3,32,128]{3,2,1,0:T(8,128)S(1)} %get-tuple-element.24), channel_id=1, source_target_pairs={{0,6},{32,70},{64,0},{96,64},{1,7},{33,71},{65,1},{97,65},{2,4},{3... | collective-permute-start | bytes 589832 | tf_op jit(solution)/shard_map/ppermute | solution.py:80
  20.1 4.9 %collective-permute-start.3 = (f32[4,3,32,128]{3,2,1,0:T(8,128)S(1)}, f32[4,3,32,128]{3,2,1,0:T(8,128)S(1)}, u32[]{:S(2)}, u32[]{:S(2)}) collective-permute-start(f32[4,3,32,128]{3,2,1,0:T(8,128)S(1)} %get-tuple-element.21), channel_id=1, source_target_pairs={{0,70},{32,6},{64,64},{96,0},{1,71},{33,7},{65,65},{97,1},{2,68},{... | collective-permute-start | bytes 589832 | tf_op jit(solution)/shard_map/ppermute | solution.py:80
  25.1 1.6 %collective-permute-start.7 = (f32[4,12,32,128]{3,2,1,0:T(8,128)S(1)}, f32[4,12,32,128]{3,2,1,0:T(8,128)S(1)}, u32[]{:S(2)}, u32[]{:S(2)}) collective-permute-start(f32[4,12,32,128]{3,2,1,0:T(8,128)S(1)} %pad_maximum_fusion.pot), channel_id=1, source_target_pairs={{0,56},{32,8},{64,120},{96,72},{1,57},{33,9},{65,121},{97,73},{2,5... | collective-permute-start | bytes 2359304 | tf_op jit(solution)/shard_map/ppermute | solution.py:80
  26.7 1.4 %collective-permute-start.8 = (f32[4,12,32,128]{3,2,1,0:T(8,128)S(1)}, f32[4,12,32,128]{3,2,1,0:T(8,128)S(1)}, u32[]{:S(2)}, u32[]{:S(2)}) collective-permute-start(f32[4,12,32,128]{3,2,1,0:T(8,128)S(1)} %pad_maximum_fusion.pot), channel_id=1, source_target_pairs={{0,32},{32,0},{64,96},{96,64},{1,33},{33,1},{65,97},{97,65},{2,34}... | collective-permute-start | bytes 2359304 | tf_op jit(solution)/shard_map/ppermute | solution.py:80
  28.1 2.8 %collective-permute-done.3.fourth = f32[4,3,32,128]{3,2,1,0:T(8,128)S(1)} collective-permute-done((f32[4,3,32,128]{3,2,1,0:T(8,128)S(1)}, f32[4,3,32,128]{3,2,1,0:T(8,128)S(1)}, u32[]{:S(2)}, u32[]{:S(2)}) %collective-permute-start.3) | collective-permute-done | bytes 196640 | tf_op jit(solution)/shard_map/ppermute | solution.py:80
  30.8 1.6 %shard_map.55 = f32[16,3,32,128]{3,2,1,0:T(8,128)S(1)} custom-call(f32[16,16]{1,0:T(8,128)S(1)} %copy-done.2, f32[4,3,32,128]{3,2,1,0:T(8,128)S(1)} %collective-permute-done.first, f32[4,3,32,128]{3,2,1,0:T(8,128)S(1)} %collective-permute-done.1.second, f32[4,3,32,128]{3,2,1,0:T(8,128)S(1)} %collective-permute-done.2.third, ...), custom_call_target="tpu_custom_call" | custom-call | flops 4194304 | bytes 1573888 | tf_op jit(solution)/shard_map/pallas_call | solution.py:221
  32.4 14.6 %all_to_all.5.own = f32[16,3,32,128]{3,2,1,0:T(8,128)S(1)} all-to-all(f32[16,3,32,128]{3,2,1,0:T(8,128)S(1)} %shard_map.55), channel_id=1, replica_groups={{64,65,66,67,68,69,70,71,0,1,2,3,4,5,6,7},{96,97,98,99,100,101,102,103,..., dimensions={0} | all-to-all | bytes 1572864 | tf_op jit(solution)/shard_map/all_to_all | solution.py:254
  47.0 4.0 %collective-permute-start.9 = (f32[16,3,32,128]{3,2,1,0:T(8,128)S(1)}, f32[16,3,32,128]{3,2,1,0:T(8,128)S(1)}, u32[]{:S(2)}, u32[]{:S(2)}) collective-permute-start(f32[16,3,32,128]{3,2,1,0:T(8,128)S(1)} %all_to_all.5.own), channel_id=1, source_target_pairs={{0,32},{32,0},{64,96},{96,64},{1,33},{33,1},{65,97},{97,65},{2,34}... | collective-permute-start | bytes 2359304 | tf_op jit(solution)/shard_map/ppermute | solution.py:80
  51.0 1.1 %collective-permute-start.10 = (f32[16,3,32,128]{3,2,1,0:T(8,128)S(1)}, f32[16,3,32,128]{3,2,1,0:T(8,128)S(1)}, u32[]{:S(2)}, u32[]{:S(2)}) collective-permute-start(f32[16,3,32,128]{3,2,1,0:T(8,128)S(1)} %all_to_all.5.own), channel_id=1, source_target_pairs={{0,56},{32,8},{64,120},{96,72},{1,57},{33,9},{65,121},{97,73},{2,5... | collective-permute-start | bytes 2359304 | tf_op jit(solution)/shard_map/ppermute | solution.py:80
  52.9 6.8 %shard_map.56 = (f32[54,32,128]{2,1,0:T(8,128)S(1)}, f32[54,32,128]{2,1,0:T(8,128)S(1)}, f32[48,32,128]{2,1,0:T(8,128)S(1)}) custom-call(f32[16,3,32,128]{3,2,1,0:T(8,128)S(1)} %all_to_all.5.own, f32[16,3,32,128]{3,2,1,0:T(8,128)S(1)} %collective-permute-done.9.other, f32[4,12,32,128]{3,2,1,0:T(8,128)S(1)} %pad_maximum_fusion.pot, ...), custom_call_target="tpu_custom_call" | custom-call | flops 536870912 | bytes 5976064 | tf_op jit(solution)/shard_map/pallas_call | solution.py:221
  59.8 3.0 %collective-permute-done.10.halo = f32[16,3,32,128]{3,2,1,0:T(8,128)S(1)} collective-permute-done((f32[16,3,32,128]{3,2,1,0:T(8,128)S(1)}, f32[16,3,32,128]{3,2,1,0:T(8,128)S(1)}, u32[]{:S(2)}, u32[]{:S(2)}) %collective-permute-start.10) | collective-permute-done | bytes 786464 | tf_op jit(solution)/shard_map/ppermute | solution.py:80
  62.7 6.8 %shard_map.57 = f32[4,12,32,128]{3,2,1,0:T(8,128)S(1)} custom-call(f32[54,32,128]{2,1,0:T(8,128)S(1)} %get-tuple-element.13.even_in, f32[54,32,128]{2,1,0:T(8,128)S(1)} %get-tuple-element.14.odd_in, f32[48,32,128]{2,1,0:T(8,128)S(1)} %get-tuple-element.15.w_in, f32[16,3,32,128]{3,2,1,0:T(8,128)S(1)} %collective-permute-done.10.halo, ...), custom_call_target="tpu_custom_call" | custom-call | flops 536870912 | bytes 5189632 | tf_op jit(solution)/shard_map/pallas_call | solution.py:221
  69.6 2.9 %collective-permute-start.11 = (f32[12,32,128]{2,1,0:T(8,128)S(1)}, f32[12,32,128]{2,1,0:T(8,128)S(1)}, u32[]{:S(2)}, u32[]{:S(2)}) collective-permute-start(f32[12,32,128]{2,1,0:T(8,128)S(1)} %get-tuple-element.20), channel_id=1, source_target_pairs={{0,64},{32,68},{64,0},{96,4},{1,65},{33,69},{65,1},{97,5},{2,66},{... | collective-permute-start | bytes 589832 | tf_op jit(solution)/shard_map/ppermute | solution.py:80
  72.5 1.4 %collective-permute-start.12 = (f32[12,32,128]{2,1,0:T(8,128)S(1)}, f32[12,32,128]{2,1,0:T(8,128)S(1)}, u32[]{:S(2)}, u32[]{:S(2)}) collective-permute-start(f32[12,32,128]{2,1,0:T(8,128)S(1)} %get-tuple-element.19), channel_id=1, source_target_pairs={{0,65},{32,69},{64,1},{96,5},{1,64},{33,68},{65,0},{97,4},{2,67},{... | collective-permute-start | bytes 589832 | tf_op jit(solution)/shard_map/ppermute | solution.py:80
  73.9 1.7 %collective-permute-start.13 = (f32[12,32,128]{2,1,0:T(8,128)S(1)}, f32[12,32,128]{2,1,0:T(8,128)S(1)}, u32[]{:S(2)}, u32[]{:S(2)}) collective-permute-start(f32[12,32,128]{2,1,0:T(8,128)S(1)} %get-tuple-element.18), channel_id=1, source_target_pairs={{0,66},{32,70},{64,2},{96,6},{1,67},{33,71},{65,3},{97,7},{2,64},{... | collective-permute-start | bytes 589832 | tf_op jit(solution)/shard_map/ppermute | solution.py:80
  75.6 2.7 %collective-permute-start.14 = (f32[12,32,128]{2,1,0:T(8,128)S(1)}, f32[12,32,128]{2,1,0:T(8,128)S(1)}, u32[]{:S(2)}, u32[]{:S(2)}) collective-permute-start(f32[12,32,128]{2,1,0:T(8,128)S(1)} %get-tuple-element.17), channel_id=1, source_target_pairs={{0,67},{32,71},{64,3},{96,7},{1,66},{33,70},{65,2},{97,6},{2,65},{... | collective-permute-start | bytes 589832 | tf_op jit(solution)/shard_map/ppermute | solution.py:80
  79.4 5.0 %collective-permute-done.12 = f32[12,32,128]{2,1,0:T(8,128)S(1)} collective-permute-done((f32[12,32,128]{2,1,0:T(8,128)S(1)}, f32[12,32,128]{2,1,0:T(8,128)S(1)}, u32[]{:S(2)}, u32[]{:S(2)}) %collective-permute-start.12) | collective-permute-done | bytes 196640 | tf_op jit(solution)/shard_map/ppermute | solution.py:80
  84.5 2.1 %collective-permute-done.14 = f32[12,32,128]{2,1,0:T(8,128)S(1)} collective-permute-done((f32[12,32,128]{2,1,0:T(8,128)S(1)}, f32[12,32,128]{2,1,0:T(8,128)S(1)}, u32[]{:S(2)}, u32[]{:S(2)}) %collective-permute-start.14) | collective-permute-done | bytes 196640 | tf_op jit(solution)/shard_map/ppermute | solution.py:80
  (30 shorter events, 3.0 us)
Async XLA Ops:
  0.0 14.8 %copy-start.3 = (f32[4,12,32,128]{3,2,1,0:T(8,128)S(1)}, f32[4,12,32,128]{3,2,1,0:T(8,128)}, u32[]{:S(2)}) copy-start(f32[4,12,32,128]{3,2,1,0:T(8,128)} %param.5) | copy-start | bytes 2359300
  0.0 9.3 %collective-permute-start.4 = (f32[12,32,128]{2,1,0:T(8,128)}, f32[12,32,128]{2,1,0:T(8,128)S(1)}, u32[]{:S(2)}, u32[]{:S(2)}) collective-permute-start(f32[12,32,128]{2,1,0:T(8,128)} %param.6), channel_id=1, source_target_pairs={{0,6},{64,70},{1,7},{65,71},{2,4},{66,68},{3,5},{67,69},{36,34},{1... | collective-permute-start | bytes 589832 | tf_op jit(solution)/shard_map/ppermute | solution.py:80
  1.4 9.9 %collective-permute-start.5 = (f32[12,32,128]{2,1,0:T(8,128)}, f32[12,32,128]{2,1,0:T(8,128)S(1)}, u32[]{:S(2)}, u32[]{:S(2)}) collective-permute-start(f32[12,32,128]{2,1,0:T(8,128)} %param.6), channel_id=1, source_target_pairs={{0,2},{32,4},{64,66},{96,68},{1,3},{33,5},{65,67},{97,69},{2,0},{3... | collective-permute-start | bytes 589832 | tf_op jit(solution)/shard_map/ppermute | solution.py:80
  11.4 13.7 %collective-permute-start.6 = (f32[2,12,32,128]{3,2,1,0:T(8,128)S(1)}, f32[2,12,32,128]{3,2,1,0:T(8,128)S(1)}, u32[]{:S(2)}, u32[]{:S(2)}) collective-permute-start(f32[2,12,32,128]{3,2,1,0:T(8,128)S(1)} %pad_maximum_fusion.1), channel_id=1, source_target_pairs={{0,65},{32,97},{64,1},{96,33},{1,64},{33,96},{65,0},{97,32},{2,67}... | collective-permute-start | bytes 1179656 | tf_op jit(solution)/shard_map/ppermute | solution.py:80
  14.9 11.8 %collective-permute-start = (f32[4,3,32,128]{3,2,1,0:T(8,128)S(1)}, f32[4,3,32,128]{3,2,1,0:T(8,128)S(1)}, u32[]{:S(2)}, u32[]{:S(2)}) collective-permute-start(f32[4,3,32,128]{3,2,1,0:T(8,128)S(1)} %get-tuple-element.23), channel_id=1, source_target_pairs={{0,0},{32,64},{64,6},{96,70},{1,1},{33,65},{65,7},{97,71},{2,2},{3... | collective-permute-start | bytes 589832 | tf_op jit(solution)/shard_map/ppermute | solution.py:80
  18.1 10.0 %collective-permute-start.1 = (f32[4,3,32,128]{3,2,1,0:T(8,128)S(1)}, f32[4,3,32,128]{3,2,1,0:T(8,128)S(1)}, u32[]{:S(2)}, u32[]{:S(2)}) collective-permute-start(f32[4,3,32,128]{3,2,1,0:T(8,128)S(1)} %get-tuple-element.22), channel_id=1, source_target_pairs={{0,64},{32,0},{64,70},{96,6},{1,65},{33,1},{65,71},{97,7},{2,66},{... | collective-permute-start | bytes 589832 | tf_op jit(solution)/shard_map/ppermute | solution.py:80
  18.1 9.9 %collective-permute-start.2 = (f32[4,3,32,128]{3,2,1,0:T(8,128)S(1)}, f32[4,3,32,128]{3,2,1,0:T(8,128)S(1)}, u32[]{:S(2)}, u32[]{:S(2)}) collective-permute-start(f32[4,3,32,128]{3,2,1,0:T(8,128)S(1)} %get-tuple-element.24), channel_id=1, source_target_pairs={{0,6},{32,70},{64,0},{96,64},{1,7},{33,71},{65,1},{97,65},{2,4},{3... | collective-permute-start | bytes 589832 | tf_op jit(solution)/shard_map/ppermute | solution.py:80
  20.1 10.7 %copy-start.2 = (f32[16,16]{1,0:T(8,128)S(1)}, f32[16,16]{1,0:T(8,128)}, u32[]{:S(2)}) copy-start(f32[16,16]{1,0:T(8,128)} %rotation.1) | copy-start | bytes 3076
  20.1 10.7 %collective-permute-start.3 = (f32[4,3,32,128]{3,2,1,0:T(8,128)S(1)}, f32[4,3,32,128]{3,2,1,0:T(8,128)S(1)}, u32[]{:S(2)}, u32[]{:S(2)}) collective-permute-start(f32[4,3,32,128]{3,2,1,0:T(8,128)S(1)} %get-tuple-element.21), channel_id=1, source_target_pairs={{0,70},{32,6},{64,64},{96,0},{1,71},{33,7},{65,65},{97,1},{2,68},{... | collective-permute-start | bytes 589832 | tf_op jit(solution)/shard_map/ppermute | solution.py:80
  25.1 21.9 %collective-permute-start.7 = (f32[4,12,32,128]{3,2,1,0:T(8,128)S(1)}, f32[4,12,32,128]{3,2,1,0:T(8,128)S(1)}, u32[]{:S(2)}, u32[]{:S(2)}) collective-permute-start(f32[4,12,32,128]{3,2,1,0:T(8,128)S(1)} %pad_maximum_fusion.pot), channel_id=1, source_target_pairs={{0,56},{32,8},{64,120},{96,72},{1,57},{33,9},{65,121},{97,73},{2,5... | collective-permute-start | bytes 2359304 | tf_op jit(solution)/shard_map/ppermute | solution.py:80
  26.7 20.3 %collective-permute-start.8 = (f32[4,12,32,128]{3,2,1,0:T(8,128)S(1)}, f32[4,12,32,128]{3,2,1,0:T(8,128)S(1)}, u32[]{:S(2)}, u32[]{:S(2)}) collective-permute-start(f32[4,12,32,128]{3,2,1,0:T(8,128)S(1)} %pad_maximum_fusion.pot), channel_id=1, source_target_pairs={{0,32},{32,0},{64,96},{96,64},{1,33},{33,1},{65,97},{97,65},{2,34}... | collective-permute-start | bytes 2359304 | tf_op jit(solution)/shard_map/ppermute | solution.py:80
  32.4 20.6 %copy-start = (bf16[256,256]{1,0:T(8,128)(2,1)S(1)}, bf16[256,256]{1,0:T(8,128)(2,1)}, u32[]{:S(2)}) copy-start(bf16[256,256]{1,0:T(8,128)(2,1)} %constant.76.clone.zmat) | copy-start | bytes 393220
  32.4 20.6 %copy-start.1 = (bf16[32,96]{1,0:T(8,128)(2,1)S(1)}, bf16[32,96]{1,0:T(8,128)(2,1)}, u32[]{:S(2)}) copy-start(bf16[32,96]{1,0:T(8,128)(2,1)} %constant.77.clone.ymat) | copy-start | bytes 18436
  47.0 6.0 %collective-permute-start.9 = (f32[16,3,32,128]{3,2,1,0:T(8,128)S(1)}, f32[16,3,32,128]{3,2,1,0:T(8,128)S(1)}, u32[]{:S(2)}, u32[]{:S(2)}) collective-permute-start(f32[16,3,32,128]{3,2,1,0:T(8,128)S(1)} %all_to_all.5.own), channel_id=1, source_target_pairs={{0,32},{32,0},{64,96},{96,64},{1,33},{33,1},{65,97},{97,65},{2,34}... | collective-permute-start | bytes 2359304 | tf_op jit(solution)/shard_map/ppermute | solution.py:80
  51.0 11.7 %collective-permute-start.10 = (f32[16,3,32,128]{3,2,1,0:T(8,128)S(1)}, f32[16,3,32,128]{3,2,1,0:T(8,128)S(1)}, u32[]{:S(2)}, u32[]{:S(2)}) collective-permute-start(f32[16,3,32,128]{3,2,1,0:T(8,128)S(1)} %all_to_all.5.own), channel_id=1, source_target_pairs={{0,56},{32,8},{64,120},{96,72},{1,57},{33,9},{65,121},{97,73},{2,5... | collective-permute-start | bytes 2359304 | tf_op jit(solution)/shard_map/ppermute | solution.py:80
  69.6 9.7 %collective-permute-start.11 = (f32[12,32,128]{2,1,0:T(8,128)S(1)}, f32[12,32,128]{2,1,0:T(8,128)S(1)}, u32[]{:S(2)}, u32[]{:S(2)}) collective-permute-start(f32[12,32,128]{2,1,0:T(8,128)S(1)} %get-tuple-element.20), channel_id=1, source_target_pairs={{0,64},{32,68},{64,0},{96,4},{1,65},{33,69},{65,1},{97,5},{2,66},{... | collective-permute-start | bytes 589832 | tf_op jit(solution)/shard_map/ppermute | solution.py:80
  72.5 11.9 %collective-permute-start.12 = (f32[12,32,128]{2,1,0:T(8,128)S(1)}, f32[12,32,128]{2,1,0:T(8,128)S(1)}, u32[]{:S(2)}, u32[]{:S(2)}) collective-permute-start(f32[12,32,128]{2,1,0:T(8,128)S(1)} %get-tuple-element.19), channel_id=1, source_target_pairs={{0,65},{32,69},{64,1},{96,5},{1,64},{33,68},{65,0},{97,4},{2,67},{... | collective-permute-start | bytes 589832 | tf_op jit(solution)/shard_map/ppermute | solution.py:80
  73.9 10.5 %collective-permute-start.13 = (f32[12,32,128]{2,1,0:T(8,128)S(1)}, f32[12,32,128]{2,1,0:T(8,128)S(1)}, u32[]{:S(2)}, u32[]{:S(2)}) collective-permute-start(f32[12,32,128]{2,1,0:T(8,128)S(1)} %get-tuple-element.18), channel_id=1, source_target_pairs={{0,66},{32,70},{64,2},{96,6},{1,67},{33,71},{65,3},{97,7},{2,64},{... | collective-permute-start | bytes 589832 | tf_op jit(solution)/shard_map/ppermute | solution.py:80
  75.6 11.0 %collective-permute-start.14 = (f32[12,32,128]{2,1,0:T(8,128)S(1)}, f32[12,32,128]{2,1,0:T(8,128)S(1)}, u32[]{:S(2)}, u32[]{:S(2)}) collective-permute-start(f32[12,32,128]{2,1,0:T(8,128)S(1)} %get-tuple-element.17), channel_id=1, source_target_pairs={{0,67},{32,71},{64,3},{96,7},{1,66},{33,70},{65,2},{97,6},{2,65},{... | collective-permute-start | bytes 589832 | tf_op jit(solution)/shard_map/ppermute | solution.py:80
  84.5 2.1 %copy-start.4 = (f32[4,12,32,128]{3,2,1,0:T(8,128)}, f32[4,12,32,128]{3,2,1,0:T(8,128)S(1)}, u32[]{:S(2)}) copy-start(f32[4,12,32,128]{3,2,1,0:T(8,128)S(1)} %bitcast_dynamic-update-slice_fusion.1) | copy-start | bytes 2359300
where the time goes:
time: 87.6 us; the launch traced here: 87.3 us
  starting transfers between devices  36.1 us (41%)
  waiting for transfers between devices  20.2 us (23%)
  Pallas kernels  15.2 us (17%)
  blocking collectives  14.6 us (17%)
  local copies, waits for them, and re-layouts  0.96 us (1%)
    ppermute x15, starting transfers between devices, permute(): return lax.ppermute(array, AXES, pairs)  36.1 us
    ppermute x15, waiting for transfers between devices, permute(): return lax.ppermute(array, AXES, pairs)  20.2 us
    pallas_call x3, Pallas kernels, call(): pl.pallas_call(kernel, out_shape=outs, in_specs=specs, out_specs=vmem(len...  15.2 us
    all_to_all x1, blocking collectives, local(): lax.all_to_all(mixed, AXES, 0, 0, tiled=True, axis_index_groups=plane_of_...  14.6 us
  transfers between devices with their start and end apart: 15, of which 8 were waited for; matrix products, arithmetic and copies ran while one was open for 0% of the time, Pallas kernels for 10%

commit v1 on v0

--- a/solution.py
+++ b/solution.py
@@ -29,7 +29,7 @@
 POT_SCALE = 2.0 / HALF_WIDTH
 BF16, F32 = jnp.bfloat16, jnp.float32
 AXES = ("band", "space")
-VMEM_LIMIT = 48 * 1024 * 1024
+VMEM_LIMIT = 16 * 1024 * 1024
 
 
 def split_gain(j):
@@ -105,6 +105,9 @@
     return [runs.index(run) for run in range(16)]
 
 
+HALVES = [[j for j, (y, z) in enumerate(HOSTS) if low_slab(y, 0) == far] for far in range(2)]
+
+
 def place():
     band, space = lax.axis_index("band"), lax.axis_index("space")
     return band // 2, band % 2, (space // 2) % 4, space % 2
@@ -112,14 +115,14 @@
 
 def mix_kernel(rotation, first, second, third, fourth, out):
     lo, core, y, hi = place()
-    mine = (y // 2) * 2 + lo
     for c in range(0, 16, 2):
         totals = [None, None]
         for r, ref in enumerate((first, second, third, fourth)):
+            band = 2 * (lo ^ (r & 1)) + ((r >> 1) ^ (y // 2) ^ core)
             for i in range(4):
                 cells = ref[i]
                 for d in range(2):
-                    term = rotation[4 * (r ^ mine) + i, c + d] * cells
+                    term = rotation[4 * band + i, c + d] * cells
                     totals[d] = term if totals[d] is None else totals[d] + term
         for d in range(2):
             out[c + d] = totals[d]
@@ -163,8 +166,8 @@
             to[at + RUN * s + t] = ref[source, jnp.where(core == 1, t, RUN - 1 - t)]
 
 
-def lay_potential(ref, to, at, core, core_from, y, hi):
-    for s in range(4):
+def lay_potential(ref, to, at, core, core_from, y, hi, slabs=4):
+    for s in range(slabs):
         slab = jnp.where(core == 1, s, 3 - s)
         source = ((slab & 1) ^ hi) * 2 + ((slab >> 1) ^ low_slab(y, core_from))
         for t in range(SLAB):
@@ -187,19 +190,47 @@
     w_out[...] = w[SEG:]
 
 
-def second_kernel(even_in, odd_in, w_in, halo, pot, zmat, ymat, out, even, odd, w):
+def lay_half(ref, to, at, core, half):
+    ahead, back = source_of_run(0), source_of_run(1)
+    for s in range(8):
+        slots = [HALVES[half].index(table) for table in (ahead[8 * half + s], back[15 - 8 * half - s])]
+        source = jnp.where(core == 1, *slots)
+        for t in range(RUN):
+            to[at + RUN * s + t] = ref[source, jnp.where(core == 1, t, RUN - 1 - t)]
+
+
+NEAR = 3 * SEG - SEG // 2
+
+
+def second_kernel(even_in, odd_in, w_in, halo, pot, zmat, ymat, even_out, odd_out, even, odd, w):
     lo, core, y, hi = place()
     shift = KEPT
     even[0 : 2 * SEG - shift] = even_in[...]
     odd[0 : 2 * SEG - shift] = odd_in[...]
     w[0:SEG] = w_in[...]
-    lay_segment(halo, even, 2 * SEG - shift, core, False)
+    lay_half(halo, even, 2 * SEG - shift, core, 0)
+    lay_potential(pot, w, SEG, core, 1 - core, y, hi, 2)
+    for k in range(1, DEGREE + 1):
+        a, b = (even, odd) if k % 2 else (odd, even)
+        for at in range(2 * SEG - RADIUS * k, NEAR - RADIUS * k, SLAB):
+            block(a, b, w, SEG - shift, zmat, ymat, at - shift, k == 1)
+    even_out[...] = even[RADIUS:]
+    odd_out[...] = odd[RADIUS:]
+
+
+def third_kernel(even_in, odd_in, w_in, halo, pot, zmat, ymat, out, even, odd, w):
+    lo, core, y, hi = place()
+    shift = SEG
+    even[0 : NEAR - shift] = even_in[...]
+    odd[0 : NEAR - shift] = odd_in[...]
+    w[SEG // 2 : SEG] = w_in[SEG // 2 :]
+    lay_half(halo, even, NEAR - shift, core, 1)
     lay_potential(pot, w, SEG, core, 1 - core, y, hi)
     for k in range(1, DEGREE + 1):
         a, b = (even, odd) if k % 2 else (odd, even)
-        for at in range(2 * SEG - RADIUS * k, 3 * SEG - RADIUS * k, SLAB):
+        for at in range(NEAR - RADIUS * k, 3 * SEG - RADIUS * k, SLAB):
             block(a, b, w, SEG - shift, zmat, ymat, at - shift, k == 1)
-    mine = (y % 2) * 2 + hi
+    mine = ((y % 2) ^ (y // 2) ^ core) * 2 + hi
     for s in range(4):
         slot = jnp.where(core == 1, s, 3 - s) ^ mine
         for t in range(SLAB):
@@ -229,24 +260,26 @@
     )(*operands)
 
 
-def spread_run(orbitals, band, r):
+def spread_run(cells, r):
     def to_run(x, y, z, c):
-        run = r ^ (2 * (z % 2) + c)
-        far, core = run >> 1, y // 2
-        return (x, 2 * far + ((y % 2) ^ core ^ far), 2 * (z // 2) + (run & 1), core)
-
-    return permute(lax.dynamic_slice_in_dim(orbitals, RUN * (r ^ band), RUN, 1), to_run)
+        far, core = (r >> 1) ^ c ^ (y // 2), y // 2
+        return (x, y if far == core else 3 - y, z ^ (r & 1), core)
+
+    return permute(cells, to_run)
 
 
 def local(orbitals, potential, rotation):
     lo, core, y, hi = place()
-    groups = [spread_run(orbitals, 2 * lo + core, r) for r in range(4)]
+    runs = [2 * ((r >> 1) ^ core ^ (y // 2)) + (lo ^ (r & 1)) for r in range(4)]
+    cells = [lax.dynamic_slice_in_dim(orbitals, RUN * run, RUN, 1) for run in runs]
     near = permute(potential, lambda x, y, z, c: (x, 3 - y, z, c) if c == y // 2 else None)
+    far = permute(potential, lambda x, y, z, c: (x, y ^ 1 if c == y // 2 else y ^ 2, z, y // 2))
+    near, *cells = lax.optimization_barrier((near, *cells))
     near = jnp.where(core == y // 2, potential, near)
-    far = permute(potential, lambda x, y, z, c: (x, y ^ 1 if c == y // 2 else y ^ 2, z, y // 2))
     pair = jnp.stack([near, far])
     next_z = permute(pair, lambda x, y, z, c: (x, y, 3 - z, c))
     pot = jnp.concatenate([pair, next_z])
+    groups = [spread_run(part, r) for r, part in enumerate(cells)]
     (mixed,) = call(mix_kernel, [planes(16, RUN)], [], 1 << 22, rotation, *groups, scalars=1)
     pot_halo = permute(pot, x_neighbour)
     pot_other = permute(pot, other_core)
@@ -254,7 +287,7 @@
     own = lax.all_to_all(mixed, AXES, 0, 0, tiled=True, axis_index_groups=plane_of_hosts)
     own, pot_halo, pot_other = lax.optimization_barrier((own, pot_halo, pot_other))
     other = permute(own, other_core)
-    halo = permute(own, x_neighbour)
+    halo = [permute(jnp.stack([own[j] for j in half]), x_neighbour) for half in HALVES]
 
     zmat, ymat = jnp.asarray(z_matrix()), jnp.asarray(y_matrix())
     kept = 2 * SEG - KEPT
@@ -270,26 +303,39 @@
         zmat,
         ymat,
     )
-    (filtered,) = call(
+    even, odd = call(
         second_kernel,
-        [planes(4, SLAB)],
-        [3 * SEG - KEPT, 3 * SEG - KEPT, 2 * SEG],
-        1 << 29,
+        [planes(NEAR - SEG), planes(NEAR - SEG)],
+        [NEAR - KEPT, NEAR - KEPT, 2 * SEG],
+        1 << 28,
         even,
         odd,
         w,
-        halo,
+        halo[0],
         pot_halo,
         zmat,
         ymat,
     )
+    (filtered,) = call(
+        third_kernel,
+        [planes(4, SLAB)],
+        [2 * SEG, 2 * SEG, 2 * SEG],
+        1 << 28,
+        even,
+        odd,
+        w,
+        halo[1],
+        pot_halo,
+        zmat,
+        ymat,
+    )
 
     result = jnp.zeros(orbitals.shape, F32)
-    mine = (y % 2) * 2 + hi
+    mine = ((y % 2) ^ (y // 2) ^ core) * 2 + hi
     for r in range(4):
 
         def to_owner(x, y, z, c):
-            slab = r ^ ((y % 2) * 2 + z // 2)
+            slab = r ^ (((y % 2) ^ (y // 2) ^ c) * 2 + z // 2)
             return (x, 2 * c + (slab >> 1), 2 * (slab & 1) + 1 - z % 2, y // 2)
 
         piece = permute(filtered[r], to_owner)

time: 87.6 us -> 84.5 us (0.965)
  waiting for transfers between devices: 20.2 us -> 15.4 us
  local copies, waits for them, and re-layouts: 0.96 us -> 2.24 us
    ppermute x15 -> x16, waiting for transfers between devices: 20.2 us -> 15.4 us  [permute(): return lax.ppermute(array, AXES, pairs)]
    dynamic_slice x1, local copies, waits for them, and re-layouts: 0.05 us -> 1.28 us  [local(): lax.dynamic_slice_in_dim(orbitals, RUN * run, RUN, 1)]
    ppermute x15 -> x16, starting transfers between devices: 36.1 us -> 35.4 us  [permute(): return lax.ppermute(array, AXES, pairs)]
    pallas_call x3 -> x4, Pallas kernels: 15.2 us -> 15.6 us  [call(): pl.pallas_call(kernel, out_shape=outs, in_specs=specs, out_specs=vmem(len...]
  transfers between devices with their start and end apart: 15 -> 16, of which waited for: 8 -> 7; matrix products, arithmetic and copies ran while one was open for 0% -> 2% of each run, Pallas kernels for 10% -> 14%
where the time goes in v1:
time: 84.5 us; the launch traced here: 84.3 us
  starting transfers between devices  35.4 us (42%)
  Pallas kernels  15.6 us (18%)
  waiting for transfers between devices  15.4 us (18%)
  blocking collectives  15.3 us (18%)
  local copies, waits for them, and re-layouts  2.24 us (3%)
    ppermute x16, starting transfers between devices, permute(): return lax.ppermute(array, AXES, pairs)  35.4 us
    pallas_call x4, Pallas kernels, call(): pl.pallas_call(kernel, out_shape=outs, in_specs=specs, out_specs=vmem(len...  15.6 us
    ppermute x16, waiting for transfers between devices, permute(): return lax.ppermute(array, AXES, pairs)  15.4 us
    all_to_all x1, blocking collectives, local(): lax.all_to_all(mixed, AXES, 0, 0, tiled=True, axis_index_groups=plane_of_...  15.3 us
  transfers between devices with their start and end apart: 16, of which 7 were waited for; matrix products, arithmetic and copies ran while one was open for 2% of the time, Pallas kernels for 14%

profile of v1, /device:TPU:1, one launch (start us, length us, event | category | flops | bytes accessed | tf_op | source)
XLA Modules:
  0.0 84.3 jit_solution(11704616611422622267)
XLA Ops:
  0.0 1.4 %collective-permute-start = (f32[12,32,128]{2,1,0:T(8,128)}, f32[12,32,128]{2,1,0:T(8,128)S(1)}, u32[]{:S(2)}, u32[]{:S(2)}) collective-permute-start(f32[12,32,128]{2,1,0:T(8,128)} %param.6), channel_id=1, source_target_pairs={{0,6},{64,70},{1,7},{65,71},{2,4},{66,68},{3,5},{67,69},{36,34},{1... | collective-permute-start | bytes 589832 | tf_op jit(solution)/shard_map/ppermute | solution.py:80
  1.4 4.4 %collective-permute-start.5 = (f32[12,32,128]{2,1,0:T(8,128)}, f32[12,32,128]{2,1,0:T(8,128)S(1)}, u32[]{:S(2)}, u32[]{:S(2)}) collective-permute-start(f32[12,32,128]{2,1,0:T(8,128)} %param.6), channel_id=1, source_target_pairs={{0,2},{32,4},{64,66},{96,68},{1,3},{33,5},{65,67},{97,69},{2,0},{3... | collective-permute-start | bytes 589832 | tf_op jit(solution)/shard_map/ppermute | solution.py:80
  5.8 1.3 %constant_dynamic-slice_fusion = (f32[4,3,32,128]{3,2,1,0:T(8,128)S(1)}, f32[4,3,32,128]{3,2,1,0:T(8,128)S(1)}, f32[4,3,32,128]{3,2,1,0:T(8,128)S(1)}, f32[4,3,32,128]{3,2,1,0:T(8,128)S(1)}) fusion(f32[4,12,32,128]{3,2,1,0:T(8,128)} %param.5, s32[]{:T(128)S(6)} %select_n.74, s32[]{:T(128)S(6)} %select_n.72, s32[]{:T(128)S(6)} %select_n.71, s32[]{:T(128)S(6)} %select_n.73), kind=kLoop, calls=%fused_computation.13 | loop fusion | bytes 1572880 | tf_op jit(solution)/shard_map/dynamic_slice | solution.py:274
  7.1 2.2 %collective-permute-done = f32[12,32,128]{2,1,0:T(8,128)S(1)} collective-permute-done((f32[12,32,128]{2,1,0:T(8,128)}, f32[12,32,128]{2,1,0:T(8,128)S(1)}, u32[]{:S(2)}, u32[]{:S(2)}) %collective-permute-start) | collective-permute-done | bytes 196640 | tf_op jit(solution)/shard_map/ppermute | solution.py:80
  9.4 1.9 %collective-permute-done.5 = f32[12,32,128]{2,1,0:T(8,128)S(1)} collective-permute-done((f32[12,32,128]{2,1,0:T(8,128)}, f32[12,32,128]{2,1,0:T(8,128)S(1)}, u32[]{:S(2)}, u32[]{:S(2)}) %collective-permute-start.5) | collective-permute-done | bytes 196640 | tf_op jit(solution)/shard_map/ppermute | solution.py:80
  11.4 3.5 %collective-permute-start.6 = (f32[2,12,32,128]{3,2,1,0:T(8,128)S(1)}, f32[2,12,32,128]{3,2,1,0:T(8,128)S(1)}, u32[]{:S(2)}, u32[]{:S(2)}) collective-permute-start(f32[2,12,32,128]{3,2,1,0:T(8,128)S(1)} %pad_maximum_fusion.1), channel_id=1, source_target_pairs={{0,65},{32,97},{64,1},{96,33},{1,64},{33,96},{65,0},{97,32},{2,67}... | collective-permute-start | bytes 1179656 | tf_op jit(solution)/shard_map/ppermute | solution.py:80
  14.8 5.8 %collective-permute-start.1 = (f32[4,3,32,128]{3,2,1,0:T(8,128)S(1)}, f32[4,3,32,128]{3,2,1,0:T(8,128)S(1)}, u32[]{:S(2)}, u32[]{:S(2)}) collective-permute-start(f32[4,3,32,128]{3,2,1,0:T(8,128)S(1)} %get-tuple-element.18), channel_id=1, source_target_pairs={{0,0},{32,6},{64,64},{96,70},{1,1},{33,7},{65,65},{97,71},{2,2},{3... | collective-permute-start | bytes 589832 | tf_op jit(solution)/shard_map/ppermute | solution.py:80
  20.7 1.9 %collective-permute-start.3 = (f32[4,3,32,128]{3,2,1,0:T(8,128)S(1)}, f32[4,3,32,128]{3,2,1,0:T(8,128)S(1)}, u32[]{:S(2)}, u32[]{:S(2)}) collective-permute-start(f32[4,3,32,128]{3,2,1,0:T(8,128)S(1)} %get-tuple-element.20), channel_id=1, source_target_pairs={{0,6},{32,0},{64,70},{96,64},{1,7},{33,1},{65,71},{97,65},{2,4},{3... | collective-permute-start | bytes 589832 | tf_op jit(solution)/shard_map/ppermute | solution.py:80
  23.5 4.7 %collective-permute-start.7 = (f32[4,12,32,128]{3,2,1,0:T(8,128)S(1)}, f32[4,12,32,128]{3,2,1,0:T(8,128)S(1)}, u32[]{:S(2)}, u32[]{:S(2)}) collective-permute-start(f32[4,12,32,128]{3,2,1,0:T(8,128)S(1)} %pad_maximum_fusion.pot), channel_id=1, source_target_pairs={{0,56},{32,8},{64,120},{96,72},{1,57},{33,9},{65,121},{97,73},{2,5... | collective-permute-start | bytes 2359304 | tf_op jit(solution)/shard_map/ppermute | solution.py:80
  28.9 3.0 %collective-permute-done.4.fourth = f32[4,3,32,128]{3,2,1,0:T(8,128)S(1)} collective-permute-done((f32[4,3,32,128]{3,2,1,0:T(8,128)S(1)}, f32[4,3,32,128]{3,2,1,0:T(8,128)S(1)}, u32[]{:S(2)}, u32[]{:S(2)}) %collective-permute-start.4) | collective-permute-done | bytes 196640 | tf_op jit(solution)/shard_map/ppermute | solution.py:80
  31.9 1.6 %shard_map.55 = f32[16,3,32,128]{3,2,1,0:T(8,128)S(1)} custom-call(f32[16,16]{1,0:T(8,128)S(1)} %copy-done.2, f32[4,3,32,128]{3,2,1,0:T(8,128)S(1)} %collective-permute-done.1.first, f32[4,3,32,128]{3,2,1,0:T(8,128)S(1)} %collective-permute-done.2.second, f32[4,3,32,128]{3,2,1,0:T(8,128)S(1)} %collective-permute-done.3.third, ...), custom_call_target="tpu_custom_call" | custom-call | flops 4194304 | bytes 1573888 | tf_op jit(solution)/shard_map/pallas_call | solution.py:252
  33.5 15.3 %all_to_all.5.own = f32[16,3,32,128]{3,2,1,0:T(8,128)S(1)} all-to-all(f32[16,3,32,128]{3,2,1,0:T(8,128)S(1)} %shard_map.55), channel_id=1, replica_groups={{64,65,66,67,68,69,70,71,0,1,2,3,4,5,6,7},{96,97,98,99,100,101,102,103,..., dimensions={0} | all-to-all | bytes 1572864 | tf_op jit(solution)/shard_map/all_to_all | solution.py:287
  48.8 2.1 %collective-permute-start.9 = (f32[16,3,32,128]{3,2,1,0:T(8,128)S(1)}, f32[16,3,32,128]{3,2,1,0:T(8,128)S(1)}, u32[]{:S(2)}, u32[]{:S(2)}) collective-permute-start(f32[16,3,32,128]{3,2,1,0:T(8,128)S(1)} %all_to_all.5.own), channel_id=1, source_target_pairs={{0,32},{32,0},{64,96},{96,64},{1,33},{33,1},{65,97},{97,65},{2,34}... | collective-permute-start | bytes 2359304 | tf_op jit(solution)/shard_map/ppermute | solution.py:80
  51.0 1.2 %collective-permute-start.10 = (f32[8,3,32,128]{3,2,1,0:T(8,128)S(1)}, f32[8,3,32,128]{3,2,1,0:T(8,128)S(1)}, u32[]{:S(2)}, u32[]{:S(2)}) collective-permute-start(f32[8,3,32,128]{3,2,1,0:T(8,128)S(1)} %pad_maximum_fusion.2), channel_id=1, source_target_pairs={{0,56},{32,8},{64,120},{96,72},{1,57},{33,9},{65,121},{97,73},{2,5... | collective-permute-start | bytes 1179656 | tf_op jit(solution)/shard_map/ppermute | solution.py:80
  52.2 0.9 %collective-permute-start.11 = (f32[8,3,32,128]{3,2,1,0:T(8,128)S(1)}, f32[8,3,32,128]{3,2,1,0:T(8,128)S(1)}, u32[]{:S(2)}, u32[]{:S(2)}) collective-permute-start(f32[8,3,32,128]{3,2,1,0:T(8,128)S(1)} %pad_maximum_fusion.3), channel_id=1, source_target_pairs={{0,56},{32,8},{64,120},{96,72},{1,57},{33,9},{65,121},{97,73},{2,5... | collective-permute-start | bytes 1179656 | tf_op jit(solution)/shard_map/ppermute | solution.py:80
  53.1 6.7 %shard_map.56 = (f32[54,32,128]{2,1,0:T(8,128)S(1)}, f32[54,32,128]{2,1,0:T(8,128)S(1)}, f32[48,32,128]{2,1,0:T(8,128)S(1)}) custom-call(f32[16,3,32,128]{3,2,1,0:T(8,128)S(1)} %all_to_all.5.own, f32[16,3,32,128]{3,2,1,0:T(8,128)S(1)} %collective-permute-done.9.other, f32[4,12,32,128]{3,2,1,0:T(8,128)S(1)} %pad_maximum_fusion.pot, ...), custom_call_target="tpu_custom_call" | custom-call | flops 536870912 | bytes 5976064 | tf_op jit(solution)/shard_map/pallas_call | solution.py:252
  59.8 3.8 %shard_map.57 = (f32[72,32,128]{2,1,0:T(8,128)S(1)}, f32[72,32,128]{2,1,0:T(8,128)S(1)}) custom-call(f32[54,32,128]{2,1,0:T(8,128)S(1)} %get-tuple-element.25.even_in, f32[54,32,128]{2,1,0:T(8,128)S(1)} %get-tuple-element.26.odd_in, f32[48,32,128]{2,1,0:T(8,128)S(1)} %get-tuple-element.27.w_in, f32[8,3,32,128]{3,2,1,0:T(8,128)S(1)} %collective-permute-done.10.halo, ...), custom_call_target="tpu_custom_call" | custom-call | flops 268435456 | bytes 6369280 | tf_op jit(solution)/shard_map/pallas_call | solution.py:252
  63.6 3.6 %shard_map.58 = f32[4,12,32,128]{3,2,1,0:T(8,128)S(1)} custom-call(f32[72,32,128]{2,1,0:T(8,128)S(1)} %get-tuple-element.29.even_in, f32[72,32,128]{2,1,0:T(8,128)S(1)} %get-tuple-element.30.odd_in, f32[48,32,128]{2,1,0:T(8,128)S(1)} %get-tuple-element.27.w_in, f32[8,3,32,128]{3,2,1,0:T(8,128)S(1)} %collective-permute-done.11.halo, ...), custom_call_target="tpu_custom_call" | custom-call | flops 268435456 | bytes 5386240 | tf_op jit(solution)/shard_map/pallas_call | solution.py:252
  67.2 2.3 %collective-permute-start.12 = (f32[12,32,128]{2,1,0:T(8,128)S(1)}, f32[12,32,128]{2,1,0:T(8,128)S(1)}, u32[]{:S(2)}, u32[]{:S(2)}) collective-permute-start(f32[12,32,128]{2,1,0:T(8,128)S(1)} %get-tuple-element.34), channel_id=1, source_target_pairs={{0,64},{32,70},{64,0},{96,6},{1,65},{33,71},{65,1},{97,7},{2,66},{... | collective-permute-start | bytes 589832 | tf_op jit(solution)/shard_map/ppermute | solution.py:80
  69.5 1.7 %collective-permute-start.13 = (f32[12,32,128]{2,1,0:T(8,128)S(1)}, f32[12,32,128]{2,1,0:T(8,128)S(1)}, u32[]{:S(2)}, u32[]{:S(2)}) collective-permute-start(f32[12,32,128]{2,1,0:T(8,128)S(1)} %get-tuple-element.33), channel_id=1, source_target_pairs={{0,65},{32,71},{64,1},{96,7},{1,64},{33,70},{65,0},{97,6},{2,67},{... | collective-permute-start | bytes 589832 | tf_op jit(solution)/shard_map/ppermute | solution.py:80
  71.2 1.2 %collective-permute-start.14 = (f32[12,32,128]{2,1,0:T(8,128)S(1)}, f32[12,32,128]{2,1,0:T(8,128)S(1)}, u32[]{:S(2)}, u32[]{:S(2)}) collective-permute-start(f32[12,32,128]{2,1,0:T(8,128)S(1)} %get-tuple-element.32), channel_id=1, source_target_pairs={{0,66},{32,68},{64,2},{96,4},{1,67},{33,69},{65,3},{97,5},{2,64},{... | collective-permute-start | bytes 589832 | tf_op jit(solution)/shard_map/ppermute | solution.py:80
  72.3 3.6 %collective-permute-start.15 = (f32[12,32,128]{2,1,0:T(8,128)S(1)}, f32[12,32,128]{2,1,0:T(8,128)S(1)}, u32[]{:S(2)}, u32[]{:S(2)}) collective-permute-start(f32[12,32,128]{2,1,0:T(8,128)S(1)} %get-tuple-element.31), channel_id=1, source_target_pairs={{0,67},{32,69},{64,3},{96,5},{1,66},{33,68},{65,2},{97,4},{2,65},{... | collective-permute-start | bytes 589832 | tf_op jit(solution)/shard_map/ppermute | solution.py:80
  76.1 2.6 %collective-permute-done.13 = f32[12,32,128]{2,1,0:T(8,128)S(1)} collective-permute-done((f32[12,32,128]{2,1,0:T(8,128)S(1)}, f32[12,32,128]{2,1,0:T(8,128)S(1)}, u32[]{:S(2)}, u32[]{:S(2)}) %collective-permute-start.13) | collective-permute-done | bytes 196640 | tf_op jit(solution)/shard_map/ppermute | solution.py:80
  79.3 4.2 %collective-permute-done.15 = f32[12,32,128]{2,1,0:T(8,128)S(1)} collective-permute-done((f32[12,32,128]{2,1,0:T(8,128)S(1)}, f32[12,32,128]{2,1,0:T(8,128)S(1)}, u32[]{:S(2)}, u32[]{:S(2)}) %collective-permute-start.15) | collective-permute-done | bytes 196640 | tf_op jit(solution)/shard_map/ppermute | solution.py:80
  (37 shorter events, 3.4 us)
Async XLA Ops:
  0.0 9.3 %copy-start.4 = (f32[12,32,128]{2,1,0:T(8,128)S(1)}, f32[12,32,128]{2,1,0:T(8,128)}, u32[]{:S(2)}) copy-start(f32[12,32,128]{2,1,0:T(8,128)} %param.6) | copy-start | bytes 589828
  0.0 9.3 %collective-permute-start = (f32[12,32,128]{2,1,0:T(8,128)}, f32[12,32,128]{2,1,0:T(8,128)S(1)}, u32[]{:S(2)}, u32[]{:S(2)}) collective-permute-start(f32[12,32,128]{2,1,0:T(8,128)} %param.6), channel_id=1, source_target_pairs={{0,6},{64,70},{1,7},{65,71},{2,4},{66,68},{3,5},{67,69},{36,34},{1... | collective-permute-start | bytes 589832 | tf_op jit(solution)/shard_map/ppermute | solution.py:80
  1.4 9.9 %collective-permute-start.5 = (f32[12,32,128]{2,1,0:T(8,128)}, f32[12,32,128]{2,1,0:T(8,128)S(1)}, u32[]{:S(2)}, u32[]{:S(2)}) collective-permute-start(f32[12,32,128]{2,1,0:T(8,128)} %param.6), channel_id=1, source_target_pairs={{0,2},{32,4},{64,66},{96,68},{1,3},{33,5},{65,67},{97,69},{2,0},{3... | collective-permute-start | bytes 589832 | tf_op jit(solution)/shard_map/ppermute | solution.py:80
  11.3 20.6 %copy-start.2 = (f32[16,16]{1,0:T(8,128)S(1)}, f32[16,16]{1,0:T(8,128)}, u32[]{:S(2)}) copy-start(f32[16,16]{1,0:T(8,128)} %rotation.1) | copy-start | bytes 3076
  11.4 12.1 %collective-permute-start.6 = (f32[2,12,32,128]{3,2,1,0:T(8,128)S(1)}, f32[2,12,32,128]{3,2,1,0:T(8,128)S(1)}, u32[]{:S(2)}, u32[]{:S(2)}) collective-permute-start(f32[2,12,32,128]{3,2,1,0:T(8,128)S(1)} %pad_maximum_fusion.1), channel_id=1, source_target_pairs={{0,65},{32,97},{64,1},{96,33},{1,64},{33,96},{65,0},{97,32},{2,67}... | collective-permute-start | bytes 1179656 | tf_op jit(solution)/shard_map/ppermute | solution.py:80
  14.8 13.4 %collective-permute-start.1 = (f32[4,3,32,128]{3,2,1,0:T(8,128)S(1)}, f32[4,3,32,128]{3,2,1,0:T(8,128)S(1)}, u32[]{:S(2)}, u32[]{:S(2)}) collective-permute-start(f32[4,3,32,128]{3,2,1,0:T(8,128)S(1)} %get-tuple-element.18), channel_id=1, source_target_pairs={{0,0},{32,6},{64,64},{96,70},{1,1},{33,7},{65,65},{97,71},{2,2},{3... | collective-permute-start | bytes 589832 | tf_op jit(solution)/shard_map/ppermute | solution.py:80
  20.7 7.6 %collective-permute-start.2 = (f32[4,3,32,128]{3,2,1,0:T(8,128)S(1)}, f32[4,3,32,128]{3,2,1,0:T(8,128)S(1)}, u32[]{:S(2)}, u32[]{:S(2)}) collective-permute-start(f32[4,3,32,128]{3,2,1,0:T(8,128)S(1)} %get-tuple-element.19), channel_id=1, source_target_pairs={{0,64},{32,70},{64,0},{96,6},{1,65},{33,71},{65,1},{97,7},{2,66},{... | collective-permute-start | bytes 589832 | tf_op jit(solution)/shard_map/ppermute | solution.py:80
  20.7 8.2 %collective-permute-start.3 = (f32[4,3,32,128]{3,2,1,0:T(8,128)S(1)}, f32[4,3,32,128]{3,2,1,0:T(8,128)S(1)}, u32[]{:S(2)}, u32[]{:S(2)}) collective-permute-start(f32[4,3,32,128]{3,2,1,0:T(8,128)S(1)} %get-tuple-element.20), channel_id=1, source_target_pairs={{0,6},{32,0},{64,70},{96,64},{1,7},{33,1},{65,71},{97,65},{2,4},{3... | collective-permute-start | bytes 589832 | tf_op jit(solution)/shard_map/ppermute | solution.py:80
  22.7 9.3 %collective-permute-start.4 = (f32[4,3,32,128]{3,2,1,0:T(8,128)S(1)}, f32[4,3,32,128]{3,2,1,0:T(8,128)S(1)}, u32[]{:S(2)}, u32[]{:S(2)}) collective-permute-start(f32[4,3,32,128]{3,2,1,0:T(8,128)S(1)} %get-tuple-element.21), channel_id=1, source_target_pairs={{0,70},{32,64},{64,6},{96,0},{1,71},{33,65},{65,7},{97,1},{2,68},{... | collective-permute-start | bytes 589832 | tf_op jit(solution)/shard_map/ppermute | solution.py:80
  23.5 25.2 %collective-permute-start.7 = (f32[4,12,32,128]{3,2,1,0:T(8,128)S(1)}, f32[4,12,32,128]{3,2,1,0:T(8,128)S(1)}, u32[]{:S(2)}, u32[]{:S(2)}) collective-permute-start(f32[4,12,32,128]{3,2,1,0:T(8,128)S(1)} %pad_maximum_fusion.pot), channel_id=1, source_target_pairs={{0,56},{32,8},{64,120},{96,72},{1,57},{33,9},{65,121},{97,73},{2,5... | collective-permute-start | bytes 2359304 | tf_op jit(solution)/shard_map/ppermute | solution.py:80
  28.2 20.6 %collective-permute-start.8 = (f32[4,12,32,128]{3,2,1,0:T(8,128)S(1)}, f32[4,12,32,128]{3,2,1,0:T(8,128)S(1)}, u32[]{:S(2)}, u32[]{:S(2)}) collective-permute-start(f32[4,12,32,128]{3,2,1,0:T(8,128)S(1)} %pad_maximum_fusion.pot), channel_id=1, source_target_pairs={{0,32},{32,0},{64,96},{96,64},{1,33},{33,1},{65,97},{97,65},{2,34}... | collective-permute-start | bytes 2359304 | tf_op jit(solution)/shard_map/ppermute | solution.py:80
  48.8 4.3 %collective-permute-start.9 = (f32[16,3,32,128]{3,2,1,0:T(8,128)S(1)}, f32[16,3,32,128]{3,2,1,0:T(8,128)S(1)}, u32[]{:S(2)}, u32[]{:S(2)}) collective-permute-start(f32[16,3,32,128]{3,2,1,0:T(8,128)S(1)} %all_to_all.5.own), channel_id=1, source_target_pairs={{0,32},{32,0},{64,96},{96,64},{1,33},{33,1},{65,97},{97,65},{2,34}... | collective-permute-start | bytes 2359304 | tf_op jit(solution)/shard_map/ppermute | solution.py:80
  50.9 2.2 %copy-start = (bf16[256,256]{1,0:T(8,128)(2,1)S(1)}, bf16[256,256]{1,0:T(8,128)(2,1)}, u32[]{:S(2)}) copy-start(bf16[256,256]{1,0:T(8,128)(2,1)} %constant.86.clone.zmat) | copy-start | bytes 393220
  50.9 2.2 %copy-start.1 = (bf16[32,96]{1,0:T(8,128)(2,1)S(1)}, bf16[32,96]{1,0:T(8,128)(2,1)}, u32[]{:S(2)}) copy-start(bf16[32,96]{1,0:T(8,128)(2,1)} %constant.87.clone.ymat) | copy-start | bytes 18436
  51.0 8.8 %collective-permute-start.10 = (f32[8,3,32,128]{3,2,1,0:T(8,128)S(1)}, f32[8,3,32,128]{3,2,1,0:T(8,128)S(1)}, u32[]{:S(2)}, u32[]{:S(2)}) collective-permute-start(f32[8,3,32,128]{3,2,1,0:T(8,128)S(1)} %pad_maximum_fusion.2), channel_id=1, source_target_pairs={{0,56},{32,8},{64,120},{96,72},{1,57},{33,9},{65,121},{97,73},{2,5... | collective-permute-start | bytes 1179656 | tf_op jit(solution)/shard_map/ppermute | solution.py:80
  52.2 11.4 %collective-permute-start.11 = (f32[8,3,32,128]{3,2,1,0:T(8,128)S(1)}, f32[8,3,32,128]{3,2,1,0:T(8,128)S(1)}, u32[]{:S(2)}, u32[]{:S(2)}) collective-permute-start(f32[8,3,32,128]{3,2,1,0:T(8,128)S(1)} %pad_maximum_fusion.3), channel_id=1, source_target_pairs={{0,56},{32,8},{64,120},{96,72},{1,57},{33,9},{65,121},{97,73},{2,5... | collective-permute-start | bytes 1179656 | tf_op jit(solution)/shard_map/ppermute | solution.py:80
  67.2 8.7 %collective-permute-start.12 = (f32[12,32,128]{2,1,0:T(8,128)S(1)}, f32[12,32,128]{2,1,0:T(8,128)S(1)}, u32[]{:S(2)}, u32[]{:S(2)}) collective-permute-start(f32[12,32,128]{2,1,0:T(8,128)S(1)} %get-tuple-element.34), channel_id=1, source_target_pairs={{0,64},{32,70},{64,0},{96,6},{1,65},{33,71},{65,1},{97,7},{2,66},{... | collective-permute-start | bytes 589832 | tf_op jit(solution)/shard_map/ppermute | solution.py:80
  69.5 9.1 %collective-permute-start.13 = (f32[12,32,128]{2,1,0:T(8,128)S(1)}, f32[12,32,128]{2,1,0:T(8,128)S(1)}, u32[]{:S(2)}, u32[]{:S(2)}) collective-permute-start(f32[12,32,128]{2,1,0:T(8,128)S(1)} %get-tuple-element.33), channel_id=1, source_target_pairs={{0,65},{32,71},{64,1},{96,7},{1,64},{33,70},{65,0},{97,6},{2,67},{... | collective-permute-start | bytes 589832 | tf_op jit(solution)/shard_map/ppermute | solution.py:80
  71.2 8.1 %collective-permute-start.14 = (f32[12,32,128]{2,1,0:T(8,128)S(1)}, f32[12,32,128]{2,1,0:T(8,128)S(1)}, u32[]{:S(2)}, u32[]{:S(2)}) collective-permute-start(f32[12,32,128]{2,1,0:T(8,128)S(1)} %get-tuple-element.32), channel_id=1, source_target_pairs={{0,66},{32,68},{64,2},{96,4},{1,67},{33,69},{65,3},{97,5},{2,64},{... | collective-permute-start | bytes 589832 | tf_op jit(solution)/shard_map/ppermute | solution.py:80
  72.3 11.2 %collective-permute-start.15 = (f32[12,32,128]{2,1,0:T(8,128)S(1)}, f32[12,32,128]{2,1,0:T(8,128)S(1)}, u32[]{:S(2)}, u32[]{:S(2)}) collective-permute-start(f32[12,32,128]{2,1,0:T(8,128)S(1)} %get-tuple-element.31), channel_id=1, source_target_pairs={{0,67},{32,69},{64,3},{96,5},{1,66},{33,68},{65,2},{97,4},{2,65},{... | collective-permute-start | bytes 589832 | tf_op jit(solution)/shard_map/ppermute | solution.py:80
  79.3 4.2 %copy-start.3 = (f32[4,12,32,128]{3,2,1,0:T(8,128)}, f32[4,12,32,128]{3,2,1,0:T(8,128)S(1)}, u32[]{:S(2)}) copy-start(f32[4,12,32,128]{3,2,1,0:T(8,128)S(1)} %bitcast_dynamic-update-slice_fusion.1) | copy-start | bytes 2359300

commit v2 on v1

--- a/solution.py
+++ b/solution.py
@@ -27,6 +27,7 @@
 HALF_WIDTH = 6.25
 GAINS = tuple(-c / HALF_WIDTH for c in COEFS)
 POT_SCALE = 2.0 / HALF_WIDTH
+OUTER = (5, 6)
 BF16, F32 = jnp.bfloat16, jnp.float32
 AXES = ("band", "space")
 VMEM_LIMIT = 16 * 1024 * 1024
@@ -50,7 +51,7 @@
 
 GAIN_GAP = 4.0 * sum(
     GAINS[j] - float(split_gain(j)[0]) - float(split_gain(j)[1]) for j in range(1, RADIUS + 1)
-)
+) + 2.0 * sum(GAINS[j] - float(split_gain(j)[0]) for j in OUTER)
 POT_SHIFT = (-2.0 * CENTER - 3.0 * COEFS[0]) / HALF_WIDTH + GAIN_GAP
 
 
@@ -61,7 +62,8 @@
 
 def y_matrix():
     high, low = circulant(NY)
-    return np.concatenate([high, high, low], axis=1)
+    outer = [np.eye(NY).astype(ml_dtypes.bfloat16) * split_gain(j)[0] for j in OUTER for _ in range(2)]
+    return np.concatenate([high, high, low, *outer], axis=1)
 
 
 def index_of(x, y, z, core):
@@ -131,7 +133,8 @@
 def block(a, b, w, w_at, zmat, ymat, at, first):
     n = SLAB
     u = a[at : at + n]
-    high = u.astype(BF16)
+    wide = a[at - RADIUS : at + n + RADIUS].astype(BF16)
+    high = wide[RADIUS : RADIUS + n]
     low = (u - high.astype(F32)).astype(BF16)
     both = jnp.concatenate([high.reshape(n * NY, NZ), low.reshape(n * NY, NZ)], axis=1)
     zz = jnp.dot(both, zmat[...], preferred_element_type=F32)
@@ -139,13 +142,16 @@
     ys = []
     for i in range(0, n, 2):
         rows = [jnp.concatenate([q[i], q[i + 1]], axis=1) for q in (high, low, high)]
+        for j in OUTER:
+            for q in (RADIUS + i + j, RADIUS + i - j):
+                rows.append(jnp.concatenate([wide[q], wide[q + 1]], axis=1))
         pair = jnp.dot(ymat[...], jnp.concatenate(rows, axis=0), preferred_element_type=F32)
         ys += [pair[:, :NZ], pair[:, NZ:]]
     for r in range(0, NY, 8):
         x = a[at - RADIUS : at + n + RADIUS, r : r + 8]
         total = w[at - w_at : at - w_at + n, r : r + 8] * x[RADIUS : RADIUS + n] + z[:, r : r + 8]
         total = total + jnp.stack([t[r : r + 8] for t in ys])
-        for j in range(1, RADIUS + 1):
+        for j in range(1, OUTER[0]):
             near = x[RADIUS + j : RADIUS + j + n] + x[RADIUS - j : RADIUS - j + n]
             total = total + GAINS[j] * near
         if first:

time: 84.5 us -> 83.3 us (0.986)
  Pallas kernels: 15.6 us -> 14.2 us
    pallas_call x4, Pallas kernels: 15.6 us -> 14.2 us  [call(): pl.pallas_call(kernel, out_shape=outs, in_specs=specs, out_specs=vmem(len...]
  transfers between devices with their start and end apart: 16 -> 16, of which waited for: 7 -> 8; matrix products, arithmetic and copies ran while one was open for 2% -> 2% of each run, Pallas kernels for 14% -> 13%
where the time goes in v2:
time: 83.3 us; the launch traced here: 83.1 us
  starting transfers between devices  35.4 us (42%)
  waiting for transfers between devices  15.6 us (19%)
  blocking collectives  15.3 us (18%)
  Pallas kernels  14.2 us (17%)
  local copies, waits for them, and re-layouts  2.25 us (3%)
    ppermute x16, starting transfers between devices, permute(): return lax.ppermute(array, AXES, pairs)  35.4 us
    ppermute x16, waiting for transfers between devices, permute(): return lax.ppermute(array, AXES, pairs)  15.6 us
    all_to_all x1, blocking collectives, local(): lax.all_to_all(mixed, AXES, 0, 0, tiled=True, axis_index_groups=plane_of_...  15.3 us
    pallas_call x4, Pallas kernels, call(): pl.pallas_call(kernel, out_shape=outs, in_specs=specs, out_specs=vmem(len...  14.2 us
  transfers between devices with their start and end apart: 16, of which 8 were waited for; matrix products, arithmetic and copies ran while one was open for 2% of the time, Pallas kernels for 13%

profile of v2, /device:TPU:1, one launch (start us, length us, event | category | flops | bytes accessed | tf_op | source)
XLA Modules:
  0.0 83.1 jit_solution(6641452487013147838)
XLA Ops:
  0.0 1.4 %collective-permute-start = (f32[12,32,128]{2,1,0:T(8,128)}, f32[12,32,128]{2,1,0:T(8,128)S(1)}, u32[]{:S(2)}, u32[]{:S(2)}) collective-permute-start(f32[12,32,128]{2,1,0:T(8,128)} %param.6), channel_id=1, source_target_pairs={{0,6},{64,70},{1,7},{65,71},{2,4},{66,68},{3,5},{67,69},{36,34},{1... | collective-permute-start | bytes 589832 | tf_op jit(solution)/shard_map/ppermute | solution.py:82
  1.4 4.4 %collective-permute-start.5 = (f32[12,32,128]{2,1,0:T(8,128)}, f32[12,32,128]{2,1,0:T(8,128)S(1)}, u32[]{:S(2)}, u32[]{:S(2)}) collective-permute-start(f32[12,32,128]{2,1,0:T(8,128)} %param.6), channel_id=1, source_target_pairs={{0,2},{32,4},{64,66},{96,68},{1,3},{33,5},{65,67},{97,69},{2,0},{3... | collective-permute-start | bytes 589832 | tf_op jit(solution)/shard_map/ppermute | solution.py:82
  5.8 1.3 %constant_dynamic-slice_fusion = (f32[4,3,32,128]{3,2,1,0:T(8,128)S(1)}, f32[4,3,32,128]{3,2,1,0:T(8,128)S(1)}, f32[4,3,32,128]{3,2,1,0:T(8,128)S(1)}, f32[4,3,32,128]{3,2,1,0:T(8,128)S(1)}) fusion(f32[4,12,32,128]{3,2,1,0:T(8,128)} %param.5, s32[]{:T(128)S(6)} %select_n.74, s32[]{:T(128)S(6)} %select_n.72, s32[]{:T(128)S(6)} %select_n.71, s32[]{:T(128)S(6)} %select_n.73), kind=kLoop, calls=%fused_computation.13 | loop fusion | bytes 1572880 | tf_op jit(solution)/shard_map/dynamic_slice | solution.py:280
  7.1 2.2 %collective-permute-done = f32[12,32,128]{2,1,0:T(8,128)S(1)} collective-permute-done((f32[12,32,128]{2,1,0:T(8,128)}, f32[12,32,128]{2,1,0:T(8,128)S(1)}, u32[]{:S(2)}, u32[]{:S(2)}) %collective-permute-start) | collective-permute-done | bytes 196640 | tf_op jit(solution)/shard_map/ppermute | solution.py:82
  9.4 1.9 %collective-permute-done.5 = f32[12,32,128]{2,1,0:T(8,128)S(1)} collective-permute-done((f32[12,32,128]{2,1,0:T(8,128)}, f32[12,32,128]{2,1,0:T(8,128)S(1)}, u32[]{:S(2)}, u32[]{:S(2)}) %collective-permute-start.5) | collective-permute-done | bytes 196640 | tf_op jit(solution)/shard_map/ppermute | solution.py:82
  11.4 3.5 %collective-permute-start.6 = (f32[2,12,32,128]{3,2,1,0:T(8,128)S(1)}, f32[2,12,32,128]{3,2,1,0:T(8,128)S(1)}, u32[]{:S(2)}, u32[]{:S(2)}) collective-permute-start(f32[2,12,32,128]{3,2,1,0:T(8,128)S(1)} %pad_maximum_fusion.1), channel_id=1, source_target_pairs={{0,65},{32,97},{64,1},{96,33},{1,64},{33,96},{65,0},{97,32},{2,67}... | collective-permute-start | bytes 1179656 | tf_op jit(solution)/shard_map/ppermute | solution.py:82
  14.8 5.8 %collective-permute-start.1 = (f32[4,3,32,128]{3,2,1,0:T(8,128)S(1)}, f32[4,3,32,128]{3,2,1,0:T(8,128)S(1)}, u32[]{:S(2)}, u32[]{:S(2)}) collective-permute-start(f32[4,3,32,128]{3,2,1,0:T(8,128)S(1)} %get-tuple-element.18), channel_id=1, source_target_pairs={{0,0},{32,6},{64,64},{96,70},{1,1},{33,7},{65,65},{97,71},{2,2},{3... | collective-permute-start | bytes 589832 | tf_op jit(solution)/shard_map/ppermute | solution.py:82
  20.7 1.9 %collective-permute-start.3 = (f32[4,3,32,128]{3,2,1,0:T(8,128)S(1)}, f32[4,3,32,128]{3,2,1,0:T(8,128)S(1)}, u32[]{:S(2)}, u32[]{:S(2)}) collective-permute-start(f32[4,3,32,128]{3,2,1,0:T(8,128)S(1)} %get-tuple-element.20), channel_id=1, source_target_pairs={{0,6},{32,0},{64,70},{96,64},{1,7},{33,1},{65,71},{97,65},{2,4},{3... | collective-permute-start | bytes 589832 | tf_op jit(solution)/shard_map/ppermute | solution.py:82
  23.5 4.7 %collective-permute-start.7 = (f32[4,12,32,128]{3,2,1,0:T(8,128)S(1)}, f32[4,12,32,128]{3,2,1,0:T(8,128)S(1)}, u32[]{:S(2)}, u32[]{:S(2)}) collective-permute-start(f32[4,12,32,128]{3,2,1,0:T(8,128)S(1)} %pad_maximum_fusion.pot), channel_id=1, source_target_pairs={{0,56},{32,8},{64,120},{96,72},{1,57},{33,9},{65,121},{97,73},{2,5... | collective-permute-start | bytes 2359304 | tf_op jit(solution)/shard_map/ppermute | solution.py:82
  28.9 3.0 %collective-permute-done.4.fourth = f32[4,3,32,128]{3,2,1,0:T(8,128)S(1)} collective-permute-done((f32[4,3,32,128]{3,2,1,0:T(8,128)S(1)}, f32[4,3,32,128]{3,2,1,0:T(8,128)S(1)}, u32[]{:S(2)}, u32[]{:S(2)}) %collective-permute-start.4) | collective-permute-done | bytes 196640 | tf_op jit(solution)/shard_map/ppermute | solution.py:82
  31.9 1.7 %shard_map.55 = f32[16,3,32,128]{3,2,1,0:T(8,128)S(1)} custom-call(f32[16,16]{1,0:T(8,128)S(1)} %copy-done.2, f32[4,3,32,128]{3,2,1,0:T(8,128)S(1)} %collective-permute-done.1.first, f32[4,3,32,128]{3,2,1,0:T(8,128)S(1)} %collective-permute-done.2.second, f32[4,3,32,128]{3,2,1,0:T(8,128)S(1)} %collective-permute-done.3.third, ...), custom_call_target="tpu_custom_call" | custom-call | flops 4194304 | bytes 1573888 | tf_op jit(solution)/shard_map/pallas_call | solution.py:258
  33.7 15.3 %all_to_all.5.own = f32[16,3,32,128]{3,2,1,0:T(8,128)S(1)} all-to-all(f32[16,3,32,128]{3,2,1,0:T(8,128)S(1)} %shard_map.55), channel_id=1, replica_groups={{64,65,66,67,68,69,70,71,0,1,2,3,4,5,6,7},{96,97,98,99,100,101,102,103,..., dimensions={0} | all-to-all | bytes 1572864 | tf_op jit(solution)/shard_map/all_to_all | solution.py:293
  49.0 2.1 %collective-permute-start.9 = (f32[16,3,32,128]{3,2,1,0:T(8,128)S(1)}, f32[16,3,32,128]{3,2,1,0:T(8,128)S(1)}, u32[]{:S(2)}, u32[]{:S(2)}) collective-permute-start(f32[16,3,32,128]{3,2,1,0:T(8,128)S(1)} %all_to_all.5.own), channel_id=1, source_target_pairs={{0,32},{32,0},{64,96},{96,64},{1,33},{33,1},{65,97},{97,65},{2,34}... | collective-permute-start | bytes 2359304 | tf_op jit(solution)/shard_map/ppermute | solution.py:82
  51.2 1.2 %collective-permute-start.10 = (f32[8,3,32,128]{3,2,1,0:T(8,128)S(1)}, f32[8,3,32,128]{3,2,1,0:T(8,128)S(1)}, u32[]{:S(2)}, u32[]{:S(2)}) collective-permute-start(f32[8,3,32,128]{3,2,1,0:T(8,128)S(1)} %pad_maximum_fusion.2), channel_id=1, source_target_pairs={{0,56},{32,8},{64,120},{96,72},{1,57},{33,9},{65,121},{97,73},{2,5... | collective-permute-start | bytes 1179656 | tf_op jit(solution)/shard_map/ppermute | solution.py:82
  52.4 0.9 %collective-permute-start.11 = (f32[8,3,32,128]{3,2,1,0:T(8,128)S(1)}, f32[8,3,32,128]{3,2,1,0:T(8,128)S(1)}, u32[]{:S(2)}, u32[]{:S(2)}) collective-permute-start(f32[8,3,32,128]{3,2,1,0:T(8,128)S(1)} %pad_maximum_fusion.3), channel_id=1, source_target_pairs={{0,56},{32,8},{64,120},{96,72},{1,57},{33,9},{65,121},{97,73},{2,5... | collective-permute-start | bytes 1179656 | tf_op jit(solution)/shard_map/ppermute | solution.py:82
  53.3 5.9 %shard_map.56 = (f32[54,32,128]{2,1,0:T(8,128)S(1)}, f32[54,32,128]{2,1,0:T(8,128)S(1)}, f32[48,32,128]{2,1,0:T(8,128)S(1)}) custom-call(f32[16,3,32,128]{3,2,1,0:T(8,128)S(1)} %all_to_all.5.own, f32[16,3,32,128]{3,2,1,0:T(8,128)S(1)} %collective-permute-done.9.other, f32[4,12,32,128]{3,2,1,0:T(8,128)S(1)} %pad_maximum_fusion.pot, ...), custom_call_target="tpu_custom_call" | custom-call | flops 536870912 | bytes 5992448 | tf_op jit(solution)/shard_map/pallas_call | solution.py:258
  59.2 3.3 %shard_map.57 = (f32[72,32,128]{2,1,0:T(8,128)S(1)}, f32[72,32,128]{2,1,0:T(8,128)S(1)}) custom-call(f32[54,32,128]{2,1,0:T(8,128)S(1)} %get-tuple-element.25.even_in, f32[54,32,128]{2,1,0:T(8,128)S(1)} %get-tuple-element.26.odd_in, f32[48,32,128]{2,1,0:T(8,128)S(1)} %get-tuple-element.27.w_in, f32[8,3,32,128]{3,2,1,0:T(8,128)S(1)} %collective-permute-done.10.halo, ...), custom_call_target="tpu_custom_call" | custom-call | flops 268435456 | bytes 6385664 | tf_op jit(solution)/shard_map/pallas_call | solution.py:258
  63.0 3.2 %shard_map.58 = f32[4,12,32,128]{3,2,1,0:T(8,128)S(1)} custom-call(f32[72,32,128]{2,1,0:T(8,128)S(1)} %get-tuple-element.29.even_in, f32[72,32,128]{2,1,0:T(8,128)S(1)} %get-tuple-element.30.odd_in, f32[48,32,128]{2,1,0:T(8,128)S(1)} %get-tuple-element.27.w_in, f32[8,3,32,128]{3,2,1,0:T(8,128)S(1)} %collective-permute-done.11.halo, ...), custom_call_target="tpu_custom_call" | custom-call | flops 268435456 | bytes 5402624 | tf_op jit(solution)/shard_map/pallas_call | solution.py:258
  66.3 2.0 %collective-permute-start.12 = (f32[12,32,128]{2,1,0:T(8,128)S(1)}, f32[12,32,128]{2,1,0:T(8,128)S(1)}, u32[]{:S(2)}, u32[]{:S(2)}) collective-permute-start(f32[12,32,128]{2,1,0:T(8,128)S(1)} %get-tuple-element.34), channel_id=1, source_target_pairs={{0,64},{32,70},{64,0},{96,6},{1,65},{33,71},{65,1},{97,7},{2,66},{... | collective-permute-start | bytes 589832 | tf_op jit(solution)/shard_map/ppermute | solution.py:82
  68.2 2.0 %collective-permute-start.13 = (f32[12,32,128]{2,1,0:T(8,128)S(1)}, f32[12,32,128]{2,1,0:T(8,128)S(1)}, u32[]{:S(2)}, u32[]{:S(2)}) collective-permute-start(f32[12,32,128]{2,1,0:T(8,128)S(1)} %get-tuple-element.33), channel_id=1, source_target_pairs={{0,65},{32,71},{64,1},{96,7},{1,64},{33,70},{65,0},{97,6},{2,67},{... | collective-permute-start | bytes 589832 | tf_op jit(solution)/shard_map/ppermute | solution.py:82
  71.0 3.9 %collective-permute-start.15 = (f32[12,32,128]{2,1,0:T(8,128)S(1)}, f32[12,32,128]{2,1,0:T(8,128)S(1)}, u32[]{:S(2)}, u32[]{:S(2)}) collective-permute-start(f32[12,32,128]{2,1,0:T(8,128)S(1)} %get-tuple-element.31), channel_id=1, source_target_pairs={{0,67},{32,69},{64,3},{96,5},{1,66},{33,68},{65,2},{97,4},{2,65},{... | collective-permute-start | bytes 589832 | tf_op jit(solution)/shard_map/ppermute | solution.py:82
  75.1 2.0 %collective-permute-done.13 = f32[12,32,128]{2,1,0:T(8,128)S(1)} collective-permute-done((f32[12,32,128]{2,1,0:T(8,128)S(1)}, f32[12,32,128]{2,1,0:T(8,128)S(1)}, u32[]{:S(2)}, u32[]{:S(2)}) %collective-permute-start.13) | collective-permute-done | bytes 196640 | tf_op jit(solution)/shard_map/ppermute | solution.py:82
  77.0 1.1 %collective-permute-done.14 = f32[12,32,128]{2,1,0:T(8,128)S(1)} collective-permute-done((f32[12,32,128]{2,1,0:T(8,128)S(1)}, f32[12,32,128]{2,1,0:T(8,128)S(1)}, u32[]{:S(2)}, u32[]{:S(2)}) %collective-permute-start.14) | collective-permute-done | bytes 196640 | tf_op jit(solution)/shard_map/ppermute | solution.py:82
  78.2 4.2 %collective-permute-done.15 = f32[12,32,128]{2,1,0:T(8,128)S(1)} collective-permute-done((f32[12,32,128]{2,1,0:T(8,128)S(1)}, f32[12,32,128]{2,1,0:T(8,128)S(1)}, u32[]{:S(2)}, u32[]{:S(2)}) %collective-permute-start.15) | collective-permute-done | bytes 196640 | tf_op jit(solution)/shard_map/ppermute | solution.py:82
  (37 shorter events, 4.0 us)
Async XLA Ops:
  0.0 9.3 %copy-start.4 = (f32[12,32,128]{2,1,0:T(8,128)S(1)}, f32[12,32,128]{2,1,0:T(8,128)}, u32[]{:S(2)}) copy-start(f32[12,32,128]{2,1,0:T(8,128)} %param.6) | copy-start | bytes 589828
  0.0 9.3 %collective-permute-start = (f32[12,32,128]{2,1,0:T(8,128)}, f32[12,32,128]{2,1,0:T(8,128)S(1)}, u32[]{:S(2)}, u32[]{:S(2)}) collective-permute-start(f32[12,32,128]{2,1,0:T(8,128)} %param.6), channel_id=1, source_target_pairs={{0,6},{64,70},{1,7},{65,71},{2,4},{66,68},{3,5},{67,69},{36,34},{1... | collective-permute-start | bytes 589832 | tf_op jit(solution)/shard_map/ppermute | solution.py:82
  1.4 9.9 %collective-permute-start.5 = (f32[12,32,128]{2,1,0:T(8,128)}, f32[12,32,128]{2,1,0:T(8,128)S(1)}, u32[]{:S(2)}, u32[]{:S(2)}) collective-permute-start(f32[12,32,128]{2,1,0:T(8,128)} %param.6), channel_id=1, source_target_pairs={{0,2},{32,4},{64,66},{96,68},{1,3},{33,5},{65,67},{97,69},{2,0},{3... | collective-permute-start | bytes 589832 | tf_op jit(solution)/shard_map/ppermute | solution.py:82
  11.3 20.6 %copy-start.2 = (f32[16,16]{1,0:T(8,128)S(1)}, f32[16,16]{1,0:T(8,128)}, u32[]{:S(2)}) copy-start(f32[16,16]{1,0:T(8,128)} %rotation.1) | copy-start | bytes 3076
  11.4 12.1 %collective-permute-start.6 = (f32[2,12,32,128]{3,2,1,0:T(8,128)S(1)}, f32[2,12,32,128]{3,2,1,0:T(8,128)S(1)}, u32[]{:S(2)}, u32[]{:S(2)}) collective-permute-start(f32[2,12,32,128]{3,2,1,0:T(8,128)S(1)} %pad_maximum_fusion.1), channel_id=1, source_target_pairs={{0,65},{32,97},{64,1},{96,33},{1,64},{33,96},{65,0},{97,32},{2,67}... | collective-permute-start | bytes 1179656 | tf_op jit(solution)/shard_map/ppermute | solution.py:82
  14.8 13.4 %collective-permute-start.1 = (f32[4,3,32,128]{3,2,1,0:T(8,128)S(1)}, f32[4,3,32,128]{3,2,1,0:T(8,128)S(1)}, u32[]{:S(2)}, u32[]{:S(2)}) collective-permute-start(f32[4,3,32,128]{3,2,1,0:T(8,128)S(1)} %get-tuple-element.18), channel_id=1, source_target_pairs={{0,0},{32,6},{64,64},{96,70},{1,1},{33,7},{65,65},{97,71},{2,2},{3... | collective-permute-start | bytes 589832 | tf_op jit(solution)/shard_map/ppermute | solution.py:82
  20.7 7.6 %collective-permute-start.2 = (f32[4,3,32,128]{3,2,1,0:T(8,128)S(1)}, f32[4,3,32,128]{3,2,1,0:T(8,128)S(1)}, u32[]{:S(2)}, u32[]{:S(2)}) collective-permute-start(f32[4,3,32,128]{3,2,1,0:T(8,128)S(1)} %get-tuple-element.19), channel_id=1, source_target_pairs={{0,64},{32,70},{64,0},{96,6},{1,65},{33,71},{65,1},{97,7},{2,66},{... | collective-permute-start | bytes 589832 | tf_op jit(solution)/shard_map/ppermute | solution.py:82
  20.7 8.2 %collective-permute-start.3 = (f32[4,3,32,128]{3,2,1,0:T(8,128)S(1)}, f32[4,3,32,128]{3,2,1,0:T(8,128)S(1)}, u32[]{:S(2)}, u32[]{:S(2)}) collective-permute-start(f32[4,3,32,128]{3,2,1,0:T(8,128)S(1)} %get-tuple-element.20), channel_id=1, source_target_pairs={{0,6},{32,0},{64,70},{96,64},{1,7},{33,1},{65,71},{97,65},{2,4},{3... | collective-permute-start | bytes 589832 | tf_op jit(solution)/shard_map/ppermute | solution.py:82
  22.7 9.3 %collective-permute-start.4 = (f32[4,3,32,128]{3,2,1,0:T(8,128)S(1)}, f32[4,3,32,128]{3,2,1,0:T(8,128)S(1)}, u32[]{:S(2)}, u32[]{:S(2)}) collective-permute-start(f32[4,3,32,128]{3,2,1,0:T(8,128)S(1)} %get-tuple-element.21), channel_id=1, source_target_pairs={{0,70},{32,64},{64,6},{96,0},{1,71},{33,65},{65,7},{97,1},{2,68},{... | collective-permute-start | bytes 589832 | tf_op jit(solution)/shard_map/ppermute | solution.py:82
  23.5 25.4 %collective-permute-start.7 = (f32[4,12,32,128]{3,2,1,0:T(8,128)S(1)}, f32[4,12,32,128]{3,2,1,0:T(8,128)S(1)}, u32[]{:S(2)}, u32[]{:S(2)}) collective-permute-start(f32[4,12,32,128]{3,2,1,0:T(8,128)S(1)} %pad_maximum_fusion.pot), channel_id=1, source_target_pairs={{0,56},{32,8},{64,120},{96,72},{1,57},{33,9},{65,121},{97,73},{2,5... | collective-permute-start | bytes 2359304 | tf_op jit(solution)/shard_map/ppermute | solution.py:82
  28.2 20.8 %collective-permute-start.8 = (f32[4,12,32,128]{3,2,1,0:T(8,128)S(1)}, f32[4,12,32,128]{3,2,1,0:T(8,128)S(1)}, u32[]{:S(2)}, u32[]{:S(2)}) collective-permute-start(f32[4,12,32,128]{3,2,1,0:T(8,128)S(1)} %pad_maximum_fusion.pot), channel_id=1, source_target_pairs={{0,32},{32,0},{64,96},{96,64},{1,33},{33,1},{65,97},{97,65},{2,34}... | collective-permute-start | bytes 2359304 | tf_op jit(solution)/shard_map/ppermute | solution.py:82
  49.0 4.3 %collective-permute-start.9 = (f32[16,3,32,128]{3,2,1,0:T(8,128)S(1)}, f32[16,3,32,128]{3,2,1,0:T(8,128)S(1)}, u32[]{:S(2)}, u32[]{:S(2)}) collective-permute-start(f32[16,3,32,128]{3,2,1,0:T(8,128)S(1)} %all_to_all.5.own), channel_id=1, source_target_pairs={{0,32},{32,0},{64,96},{96,64},{1,33},{33,1},{65,97},{97,65},{2,34}... | collective-permute-start | bytes 2359304 | tf_op jit(solution)/shard_map/ppermute | solution.py:82
  51.1 2.2 %copy-start = (bf16[256,256]{1,0:T(8,128)(2,1)S(1)}, bf16[256,256]{1,0:T(8,128)(2,1)}, u32[]{:S(2)}) copy-start(bf16[256,256]{1,0:T(8,128)(2,1)} %constant.86.clone.zmat) | copy-start | bytes 393220
  51.1 2.2 %copy-start.1 = (bf16[32,224]{1,0:T(8,128)(2,1)S(1)}, bf16[32,224]{1,0:T(8,128)(2,1)}, u32[]{:S(2)}) copy-start(bf16[32,224]{1,0:T(8,128)(2,1)} %constant.87.clone.ymat) | copy-start | bytes 43012
  51.2 8.0 %collective-permute-start.10 = (f32[8,3,32,128]{3,2,1,0:T(8,128)S(1)}, f32[8,3,32,128]{3,2,1,0:T(8,128)S(1)}, u32[]{:S(2)}, u32[]{:S(2)}) collective-permute-start(f32[8,3,32,128]{3,2,1,0:T(8,128)S(1)} %pad_maximum_fusion.2), channel_id=1, source_target_pairs={{0,56},{32,8},{64,120},{96,72},{1,57},{33,9},{65,121},{97,73},{2,5... | collective-permute-start | bytes 1179656 | tf_op jit(solution)/shard_map/ppermute | solution.py:82
  52.4 10.6 %collective-permute-start.11 = (f32[8,3,32,128]{3,2,1,0:T(8,128)S(1)}, f32[8,3,32,128]{3,2,1,0:T(8,128)S(1)}, u32[]{:S(2)}, u32[]{:S(2)}) collective-permute-start(f32[8,3,32,128]{3,2,1,0:T(8,128)S(1)} %pad_maximum_fusion.3), channel_id=1, source_target_pairs={{0,56},{32,8},{64,120},{96,72},{1,57},{33,9},{65,121},{97,73},{2,5... | collective-permute-start | bytes 1179656 | tf_op jit(solution)/shard_map/ppermute | solution.py:82
  66.3 8.7 %collective-permute-start.12 = (f32[12,32,128]{2,1,0:T(8,128)S(1)}, f32[12,32,128]{2,1,0:T(8,128)S(1)}, u32[]{:S(2)}, u32[]{:S(2)}) collective-permute-start(f32[12,32,128]{2,1,0:T(8,128)S(1)} %get-tuple-element.34), channel_id=1, source_target_pairs={{0,64},{32,70},{64,0},{96,6},{1,65},{33,71},{65,1},{97,7},{2,66},{... | collective-permute-start | bytes 589832 | tf_op jit(solution)/shard_map/ppermute | solution.py:82
  68.2 8.8 %collective-permute-start.13 = (f32[12,32,128]{2,1,0:T(8,128)S(1)}, f32[12,32,128]{2,1,0:T(8,128)S(1)}, u32[]{:S(2)}, u32[]{:S(2)}) collective-permute-start(f32[12,32,128]{2,1,0:T(8,128)S(1)} %get-tuple-element.33), channel_id=1, source_target_pairs={{0,65},{32,71},{64,1},{96,7},{1,64},{33,70},{65,0},{97,6},{2,67},{... | collective-permute-start | bytes 589832 | tf_op jit(solution)/shard_map/ppermute | solution.py:82
  70.2 8.0 %collective-permute-start.14 = (f32[12,32,128]{2,1,0:T(8,128)S(1)}, f32[12,32,128]{2,1,0:T(8,128)S(1)}, u32[]{:S(2)}, u32[]{:S(2)}) collective-permute-start(f32[12,32,128]{2,1,0:T(8,128)S(1)} %get-tuple-element.32), channel_id=1, source_target_pairs={{0,66},{32,68},{64,2},{96,4},{1,67},{33,69},{65,3},{97,5},{2,64},{... | collective-permute-start | bytes 589832 | tf_op jit(solution)/shard_map/ppermute | solution.py:82
  71.0 11.4 %collective-permute-start.15 = (f32[12,32,128]{2,1,0:T(8,128)S(1)}, f32[12,32,128]{2,1,0:T(8,128)S(1)}, u32[]{:S(2)}, u32[]{:S(2)}) collective-permute-start(f32[12,32,128]{2,1,0:T(8,128)S(1)} %get-tuple-element.31), channel_id=1, source_target_pairs={{0,67},{32,69},{64,3},{96,5},{1,66},{33,68},{65,2},{97,4},{2,65},{... | collective-permute-start | bytes 589832 | tf_op jit(solution)/shard_map/ppermute | solution.py:82
  78.2 4.2 %copy-start.3 = (f32[4,12,32,128]{3,2,1,0:T(8,128)}, f32[4,12,32,128]{3,2,1,0:T(8,128)S(1)}, u32[]{:S(2)}) copy-start(f32[4,12,32,128]{3,2,1,0:T(8,128)S(1)} %bitcast_dynamic-update-slice_fusion.1) | copy-start | bytes 2359300

commit v3 on v2

--- a/solution.py
+++ b/solution.py
@@ -115,11 +115,11 @@
     return band // 2, band % 2, (space // 2) % 4, space % 2
 
 
-def mix_kernel(rotation, first, second, third, fourth, out):
+def mix(rotation, parts, out, start):
     lo, core, y, hi = place()
     for c in range(0, 16, 2):
-        totals = [None, None]
-        for r, ref in enumerate((first, second, third, fourth)):
+        totals = [None, None] if start is None else [start[c], start[c + 1]]
+        for r, ref in parts:
             band = 2 * (lo ^ (r & 1)) + ((r >> 1) ^ (y // 2) ^ core)
             for i in range(4):
                 cells = ref[i]
@@ -128,6 +128,14 @@
                     totals[d] = term if totals[d] is None else totals[d] + term
         for d in range(2):
             out[c + d] = totals[d]
+
+
+def mix_kernel(rotation, first, second, third, out):
+    mix(rotation, ((0, first), (1, second), (2, third)), out, None)
+
+
+def mix_last_kernel(rotation, fourth, sums, out):
+    mix(rotation, ((3, fourth),), out, sums)
 
 
 def block(a, b, w, w_at, zmat, ymat, at, first):
@@ -286,7 +294,8 @@
     next_z = permute(pair, lambda x, y, z, c: (x, y, 3 - z, c))
     pot = jnp.concatenate([pair, next_z])
     groups = [spread_run(part, r) for r, part in enumerate(cells)]
-    (mixed,) = call(mix_kernel, [planes(16, RUN)], [], 1 << 22, rotation, *groups, scalars=1)
+    (sums,) = call(mix_kernel, [planes(16, RUN)], [], 3 << 20, rotation, *groups[:3], scalars=1)
+    (mixed,) = call(mix_last_kernel, [planes(16, RUN)], [], 1 << 20, rotation, groups[3], sums, scalars=1)
     pot_halo = permute(pot, x_neighbour)
     pot_other = permute(pot, other_core)
     plane_of_hosts = [[index_of(x, *chip, c) for chip in HOSTS] for x in range(4) for c in range(2)]

time: 83.3 us -> 82.5 us (level)
  waiting for transfers between devices: 15.6 us -> 14.3 us
    ppermute x16, waiting for transfers between devices: 15.6 us -> 14.3 us  [permute(): return lax.ppermute(array, AXES, pairs)]
    pallas_call x4 -> x5, Pallas kernels: 14.2 us -> 14.7 us  [call(): pl.pallas_call(kernel, out_shape=outs, in_specs=specs, out_specs=vmem(len...]
  transfers between devices with their start and end apart: 16 -> 16, of which waited for: 8 -> 8; matrix products, arithmetic and copies ran while one was open for 2% -> 2% of each run, Pallas kernels for 13% -> 14%
where the time goes in v3:
time: 82.5 us; the launch traced here: 82.3 us
  starting transfers between devices  35.4 us (43%)
  blocking collectives  15.3 us (19%)
  Pallas kernels  14.7 us (18%)
  waiting for transfers between devices  14.3 us (17%)
  local copies, waits for them, and re-layouts  2.23 us (3%)
    ppermute x16, starting transfers between devices, permute(): return lax.ppermute(array, AXES, pairs)  35.4 us
    all_to_all x1, blocking collectives, local(): lax.all_to_all(mixed, AXES, 0, 0, tiled=True, axis_index_groups=plane_of_...  15.3 us
    pallas_call x5, Pallas kernels, call(): pl.pallas_call(kernel, out_shape=outs, in_specs=specs, out_specs=vmem(len...  14.7 us
    ppermute x16, waiting for transfers between devices, permute(): return lax.ppermute(array, AXES, pairs)  14.3 us
  transfers between devices with their start and end apart: 16, of which 8 were waited for; matrix products, arithmetic and copies ran while one was open for 2% of the time, Pallas kernels for 14%

profile of v3, /device:TPU:1, one launch (start us, length us, event | category | flops | bytes accessed | tf_op | source)
XLA Modules:
  0.0 82.3 jit_solution(3484783078530021527)
XLA Ops:
  0.0 1.4 %collective-permute-start = (f32[12,32,128]{2,1,0:T(8,128)}, f32[12,32,128]{2,1,0:T(8,128)S(1)}, u32[]{:S(2)}, u32[]{:S(2)}) collective-permute-start(f32[12,32,128]{2,1,0:T(8,128)} %param.6), channel_id=1, source_target_pairs={{0,6},{64,70},{1,7},{65,71},{2,4},{66,68},{3,5},{67,69},{36,34},{1... | collective-permute-start | bytes 589832 | tf_op jit(solution)/shard_map/ppermute | solution.py:82
  1.4 4.4 %collective-permute-start.5 = (f32[12,32,128]{2,1,0:T(8,128)}, f32[12,32,128]{2,1,0:T(8,128)S(1)}, u32[]{:S(2)}, u32[]{:S(2)}) collective-permute-start(f32[12,32,128]{2,1,0:T(8,128)} %param.6), channel_id=1, source_target_pairs={{0,2},{32,4},{64,66},{96,68},{1,3},{33,5},{65,67},{97,69},{2,0},{3... | collective-permute-start | bytes 589832 | tf_op jit(solution)/shard_map/ppermute | solution.py:82
  5.8 1.3 %constant_dynamic-slice_fusion = (f32[4,3,32,128]{3,2,1,0:T(8,128)S(1)}, f32[4,3,32,128]{3,2,1,0:T(8,128)S(1)}, f32[4,3,32,128]{3,2,1,0:T(8,128)S(1)}, f32[4,3,32,128]{3,2,1,0:T(8,128)S(1)}) fusion(f32[4,12,32,128]{3,2,1,0:T(8,128)} %param.5, s32[]{:T(128)S(6)} %select_n.74, s32[]{:T(128)S(6)} %select_n.72, s32[]{:T(128)S(6)} %select_n.71, s32[]{:T(128)S(6)} %select_n.73), kind=kLoop, calls=%fused_computation.13 | loop fusion | bytes 1572880 | tf_op jit(solution)/shard_map/dynamic_slice | solution.py:288
  7.1 2.3 %collective-permute-done = f32[12,32,128]{2,1,0:T(8,128)S(1)} collective-permute-done((f32[12,32,128]{2,1,0:T(8,128)}, f32[12,32,128]{2,1,0:T(8,128)S(1)}, u32[]{:S(2)}, u32[]{:S(2)}) %collective-permute-start) | collective-permute-done | bytes 196640 | tf_op jit(solution)/shard_map/ppermute | solution.py:82
  9.4 1.9 %collective-permute-done.5 = f32[12,32,128]{2,1,0:T(8,128)S(1)} collective-permute-done((f32[12,32,128]{2,1,0:T(8,128)}, f32[12,32,128]{2,1,0:T(8,128)S(1)}, u32[]{:S(2)}, u32[]{:S(2)}) %collective-permute-start.5) | collective-permute-done | bytes 196640 | tf_op jit(solution)/shard_map/ppermute | solution.py:82
  11.4 3.5 %collective-permute-start.6 = (f32[2,12,32,128]{3,2,1,0:T(8,128)S(1)}, f32[2,12,32,128]{3,2,1,0:T(8,128)S(1)}, u32[]{:S(2)}, u32[]{:S(2)}) collective-permute-start(f32[2,12,32,128]{3,2,1,0:T(8,128)S(1)} %pad_maximum_fusion.1), channel_id=1, source_target_pairs={{0,65},{32,97},{64,1},{96,33},{1,64},{33,96},{65,0},{97,32},{2,67}... | collective-permute-start | bytes 1179656 | tf_op jit(solution)/shard_map/ppermute | solution.py:82
  14.8 5.8 %collective-permute-start.2 = (f32[4,3,32,128]{3,2,1,0:T(8,128)S(1)}, f32[4,3,32,128]{3,2,1,0:T(8,128)S(1)}, u32[]{:S(2)}, u32[]{:S(2)}) collective-permute-start(f32[4,3,32,128]{3,2,1,0:T(8,128)S(1)} %get-tuple-element.19), channel_id=1, source_target_pairs={{0,0},{32,6},{64,64},{96,70},{1,1},{33,7},{65,65},{97,71},{2,2},{3... | collective-permute-start | bytes 589832 | tf_op jit(solution)/shard_map/ppermute | solution.py:82
  20.7 1.9 %collective-permute-start.4 = (f32[4,3,32,128]{3,2,1,0:T(8,128)S(1)}, f32[4,3,32,128]{3,2,1,0:T(8,128)S(1)}, u32[]{:S(2)}, u32[]{:S(2)}) collective-permute-start(f32[4,3,32,128]{3,2,1,0:T(8,128)S(1)} %get-tuple-element.21), channel_id=1, source_target_pairs={{0,6},{32,0},{64,70},{96,64},{1,7},{33,1},{65,71},{97,65},{2,4},{3... | collective-permute-start | bytes 589832 | tf_op jit(solution)/shard_map/ppermute | solution.py:82
  23.5 4.7 %collective-permute-start.7 = (f32[4,12,32,128]{3,2,1,0:T(8,128)S(1)}, f32[4,12,32,128]{3,2,1,0:T(8,128)S(1)}, u32[]{:S(2)}, u32[]{:S(2)}) collective-permute-start(f32[4,12,32,128]{3,2,1,0:T(8,128)S(1)} %pad_maximum_fusion.pot), channel_id=1, source_target_pairs={{0,56},{32,8},{64,120},{96,72},{1,57},{33,9},{65,121},{97,73},{2,5... | collective-permute-start | bytes 2359304 | tf_op jit(solution)/shard_map/ppermute | solution.py:82
  28.9 1.4 %shard_map.55.sums = f32[16,3,32,128]{3,2,1,0:T(8,128)S(1)} custom-call(f32[16,16]{1,0:T(8,128)S(1)} %copy-done.2, f32[4,3,32,128]{3,2,1,0:T(8,128)S(1)} %collective-permute-done.2.first, f32[4,3,32,128]{3,2,1,0:T(8,128)S(1)} %collective-permute-done.3.second, f32[4,3,32,128]{3,2,1,0:T(8,128)S(1)} %collective-permute-done.4.third), custom_call_target="tpu_custom_call" | custom-call | flops 3145728 | bytes 1377280 | tf_op jit(solution)/shard_map/pallas_call | solution.py:266
  30.3 1.6 %collective-permute-done.1.fourth = f32[4,3,32,128]{3,2,1,0:T(8,128)S(1)} collective-permute-done((f32[4,3,32,128]{3,2,1,0:T(8,128)S(1)}, f32[4,3,32,128]{3,2,1,0:T(8,128)S(1)}, u32[]{:S(2)}, u32[]{:S(2)}) %collective-permute-start.1) | collective-permute-done | bytes 196640 | tf_op jit(solution)/shard_map/ppermute | solution.py:82
  31.9 0.9 %shard_map.56 = f32[16,3,32,128]{3,2,1,0:T(8,128)S(1)} custom-call(f32[16,16]{1,0:T(8,128)S(1)} %copy-done.2, f32[4,3,32,128]{3,2,1,0:T(8,128)S(1)} %collective-permute-done.1.fourth, f32[16,3,32,128]{3,2,1,0:T(8,128)S(1)} %shard_map.55.sums), custom_call_target="tpu_custom_call" | custom-call | flops 1048576 | bytes 1770496 | tf_op jit(solution)/shard_map/pallas_call | solution.py:266
  32.9 15.3 %all_to_all.5.own = f32[16,3,32,128]{3,2,1,0:T(8,128)S(1)} all-to-all(f32[16,3,32,128]{3,2,1,0:T(8,128)S(1)} %shard_map.56), channel_id=1, replica_groups={{64,65,66,67,68,69,70,71,0,1,2,3,4,5,6,7},{96,97,98,99,100,101,102,103,..., dimensions={0} | all-to-all | bytes 1572864 | tf_op jit(solution)/shard_map/all_to_all | solution.py:302
  48.1 2.1 %collective-permute-start.9 = (f32[16,3,32,128]{3,2,1,0:T(8,128)S(1)}, f32[16,3,32,128]{3,2,1,0:T(8,128)S(1)}, u32[]{:S(2)}, u32[]{:S(2)}) collective-permute-start(f32[16,3,32,128]{3,2,1,0:T(8,128)S(1)} %all_to_all.5.own), channel_id=1, source_target_pairs={{0,32},{32,0},{64,96},{96,64},{1,33},{33,1},{65,97},{97,65},{2,34}... | collective-permute-start | bytes 2359304 | tf_op jit(solution)/shard_map/ppermute | solution.py:82
  50.4 1.2 %collective-permute-start.10 = (f32[8,3,32,128]{3,2,1,0:T(8,128)S(1)}, f32[8,3,32,128]{3,2,1,0:T(8,128)S(1)}, u32[]{:S(2)}, u32[]{:S(2)}) collective-permute-start(f32[8,3,32,128]{3,2,1,0:T(8,128)S(1)} %pad_maximum_fusion.2), channel_id=1, source_target_pairs={{0,56},{32,8},{64,120},{96,72},{1,57},{33,9},{65,121},{97,73},{2,5... | collective-permute-start | bytes 1179656 | tf_op jit(solution)/shard_map/ppermute | solution.py:82
  52.5 5.9 %shard_map.57 = (f32[54,32,128]{2,1,0:T(8,128)S(1)}, f32[54,32,128]{2,1,0:T(8,128)S(1)}, f32[48,32,128]{2,1,0:T(8,128)S(1)}) custom-call(f32[16,3,32,128]{3,2,1,0:T(8,128)S(1)} %all_to_all.5.own, f32[16,3,32,128]{3,2,1,0:T(8,128)S(1)} %collective-permute-done.9.other, f32[4,12,32,128]{3,2,1,0:T(8,128)S(1)} %pad_maximum_fusion.pot, ...), custom_call_target="tpu_custom_call" | custom-call | flops 536870912 | bytes 5992448 | tf_op jit(solution)/shard_map/pallas_call | solution.py:266
  58.4 3.3 %shard_map.58 = (f32[72,32,128]{2,1,0:T(8,128)S(1)}, f32[72,32,128]{2,1,0:T(8,128)S(1)}) custom-call(f32[54,32,128]{2,1,0:T(8,128)S(1)} %get-tuple-element.25.even_in, f32[54,32,128]{2,1,0:T(8,128)S(1)} %get-tuple-element.26.odd_in, f32[48,32,128]{2,1,0:T(8,128)S(1)} %get-tuple-element.27.w_in, f32[8,3,32,128]{3,2,1,0:T(8,128)S(1)} %collective-permute-done.10.halo, ...), custom_call_target="tpu_custom_call" | custom-call | flops 268435456 | bytes 6385664 | tf_op jit(solution)/shard_map/pallas_call | solution.py:266
  62.2 3.2 %shard_map.59 = f32[4,12,32,128]{3,2,1,0:T(8,128)S(1)} custom-call(f32[72,32,128]{2,1,0:T(8,128)S(1)} %get-tuple-element.29.even_in, f32[72,32,128]{2,1,0:T(8,128)S(1)} %get-tuple-element.30.odd_in, f32[48,32,128]{2,1,0:T(8,128)S(1)} %get-tuple-element.27.w_in, f32[8,3,32,128]{3,2,1,0:T(8,128)S(1)} %collective-permute-done.11.halo, ...), custom_call_target="tpu_custom_call" | custom-call | flops 268435456 | bytes 5402624 | tf_op jit(solution)/shard_map/pallas_call | solution.py:266
  65.4 2.0 %collective-permute-start.12 = (f32[12,32,128]{2,1,0:T(8,128)S(1)}, f32[12,32,128]{2,1,0:T(8,128)S(1)}, u32[]{:S(2)}, u32[]{:S(2)}) collective-permute-start(f32[12,32,128]{2,1,0:T(8,128)S(1)} %get-tuple-element.34), channel_id=1, source_target_pairs={{0,64},{32,70},{64,0},{96,6},{1,65},{33,71},{65,1},{97,7},{2,66},{... | collective-permute-start | bytes 589832 | tf_op jit(solution)/shard_map/ppermute | solution.py:82
  67.4 2.0 %collective-permute-start.13 = (f32[12,32,128]{2,1,0:T(8,128)S(1)}, f32[12,32,128]{2,1,0:T(8,128)S(1)}, u32[]{:S(2)}, u32[]{:S(2)}) collective-permute-start(f32[12,32,128]{2,1,0:T(8,128)S(1)} %get-tuple-element.33), channel_id=1, source_target_pairs={{0,65},{32,71},{64,1},{96,7},{1,64},{33,70},{65,0},{97,6},{2,67},{... | collective-permute-start | bytes 589832 | tf_op jit(solution)/shard_map/ppermute | solution.py:82
  70.2 3.9 %collective-permute-start.15 = (f32[12,32,128]{2,1,0:T(8,128)S(1)}, f32[12,32,128]{2,1,0:T(8,128)S(1)}, u32[]{:S(2)}, u32[]{:S(2)}) collective-permute-start(f32[12,32,128]{2,1,0:T(8,128)S(1)} %get-tuple-element.31), channel_id=1, source_target_pairs={{0,67},{32,69},{64,3},{96,5},{1,66},{33,68},{65,2},{97,4},{2,65},{... | collective-permute-start | bytes 589832 | tf_op jit(solution)/shard_map/ppermute | solution.py:82
  74.2 2.0 %collective-permute-done.13 = f32[12,32,128]{2,1,0:T(8,128)S(1)} collective-permute-done((f32[12,32,128]{2,1,0:T(8,128)S(1)}, f32[12,32,128]{2,1,0:T(8,128)S(1)}, u32[]{:S(2)}, u32[]{:S(2)}) %collective-permute-start.13) | collective-permute-done | bytes 196640 | tf_op jit(solution)/shard_map/ppermute | solution.py:82
  76.2 1.1 %collective-permute-done.14 = f32[12,32,128]{2,1,0:T(8,128)S(1)} collective-permute-done((f32[12,32,128]{2,1,0:T(8,128)S(1)}, f32[12,32,128]{2,1,0:T(8,128)S(1)}, u32[]{:S(2)}, u32[]{:S(2)}) %collective-permute-start.14) | collective-permute-done | bytes 196640 | tf_op jit(solution)/shard_map/ppermute | solution.py:82
  77.4 4.2 %collective-permute-done.15 = f32[12,32,128]{2,1,0:T(8,128)S(1)} collective-permute-done((f32[12,32,128]{2,1,0:T(8,128)S(1)}, f32[12,32,128]{2,1,0:T(8,128)S(1)}, u32[]{:S(2)}, u32[]{:S(2)}) %collective-permute-start.15) | collective-permute-done | bytes 196640 | tf_op jit(solution)/shard_map/ppermute | solution.py:82
  (38 shorter events, 4.9 us)
Async XLA Ops:
  0.0 9.3 %copy-start.4 = (f32[12,32,128]{2,1,0:T(8,128)S(1)}, f32[12,32,128]{2,1,0:T(8,128)}, u32[]{:S(2)}) copy-start(f32[12,32,128]{2,1,0:T(8,128)} %param.6) | copy-start | bytes 589828
  0.0 9.3 %collective-permute-start = (f32[12,32,128]{2,1,0:T(8,128)}, f32[12,32,128]{2,1,0:T(8,128)S(1)}, u32[]{:S(2)}, u32[]{:S(2)}) collective-permute-start(f32[12,32,128]{2,1,0:T(8,128)} %param.6), channel_id=1, source_target_pairs={{0,6},{64,70},{1,7},{65,71},{2,4},{66,68},{3,5},{67,69},{36,34},{1... | collective-permute-start | bytes 589832 | tf_op jit(solution)/shard_map/ppermute | solution.py:82
  1.4 9.9 %collective-permute-start.5 = (f32[12,32,128]{2,1,0:T(8,128)}, f32[12,32,128]{2,1,0:T(8,128)S(1)}, u32[]{:S(2)}, u32[]{:S(2)}) collective-permute-start(f32[12,32,128]{2,1,0:T(8,128)} %param.6), channel_id=1, source_target_pairs={{0,2},{32,4},{64,66},{96,68},{1,3},{33,5},{65,67},{97,69},{2,0},{3... | collective-permute-start | bytes 589832 | tf_op jit(solution)/shard_map/ppermute | solution.py:82
  11.3 17.6 %copy-start.2 = (f32[16,16]{1,0:T(8,128)S(1)}, f32[16,16]{1,0:T(8,128)}, u32[]{:S(2)}) copy-start(f32[16,16]{1,0:T(8,128)} %rotation.3) | copy-start | bytes 3076
  11.4 12.1 %collective-permute-start.6 = (f32[2,12,32,128]{3,2,1,0:T(8,128)S(1)}, f32[2,12,32,128]{3,2,1,0:T(8,128)S(1)}, u32[]{:S(2)}, u32[]{:S(2)}) collective-permute-start(f32[2,12,32,128]{3,2,1,0:T(8,128)S(1)} %pad_maximum_fusion.1), channel_id=1, source_target_pairs={{0,65},{32,97},{64,1},{96,33},{1,64},{33,96},{65,0},{97,32},{2,67}... | collective-permute-start | bytes 1179656 | tf_op jit(solution)/shard_map/ppermute | solution.py:82
  14.8 13.4 %collective-permute-start.2 = (f32[4,3,32,128]{3,2,1,0:T(8,128)S(1)}, f32[4,3,32,128]{3,2,1,0:T(8,128)S(1)}, u32[]{:S(2)}, u32[]{:S(2)}) collective-permute-start(f32[4,3,32,128]{3,2,1,0:T(8,128)S(1)} %get-tuple-element.19), channel_id=1, source_target_pairs={{0,0},{32,6},{64,64},{96,70},{1,1},{33,7},{65,65},{97,71},{2,2},{3... | collective-permute-start | bytes 589832 | tf_op jit(solution)/shard_map/ppermute | solution.py:82
  20.7 7.6 %collective-permute-start.3 = (f32[4,3,32,128]{3,2,1,0:T(8,128)S(1)}, f32[4,3,32,128]{3,2,1,0:T(8,128)S(1)}, u32[]{:S(2)}, u32[]{:S(2)}) collective-permute-start(f32[4,3,32,128]{3,2,1,0:T(8,128)S(1)} %get-tuple-element.20), channel_id=1, source_target_pairs={{0,64},{32,70},{64,0},{96,6},{1,65},{33,71},{65,1},{97,7},{2,66},{... | collective-permute-start | bytes 589832 | tf_op jit(solution)/shard_map/ppermute | solution.py:82
  20.7 8.2 %collective-permute-start.4 = (f32[4,3,32,128]{3,2,1,0:T(8,128)S(1)}, f32[4,3,32,128]{3,2,1,0:T(8,128)S(1)}, u32[]{:S(2)}, u32[]{:S(2)}) collective-permute-start(f32[4,3,32,128]{3,2,1,0:T(8,128)S(1)} %get-tuple-element.21), channel_id=1, source_target_pairs={{0,6},{32,0},{64,70},{96,64},{1,7},{33,1},{65,71},{97,65},{2,4},{3... | collective-permute-start | bytes 589832 | tf_op jit(solution)/shard_map/ppermute | solution.py:82
  22.7 9.3 %collective-permute-start.1 = (f32[4,3,32,128]{3,2,1,0:T(8,128)S(1)}, f32[4,3,32,128]{3,2,1,0:T(8,128)S(1)}, u32[]{:S(2)}, u32[]{:S(2)}) collective-permute-start(f32[4,3,32,128]{3,2,1,0:T(8,128)S(1)} %get-tuple-element.18), channel_id=1, source_target_pairs={{0,70},{32,64},{64,6},{96,0},{1,71},{33,65},{65,7},{97,1},{2,68},{... | collective-permute-start | bytes 589832 | tf_op jit(solution)/shard_map/ppermute | solution.py:82
  23.5 24.6 %collective-permute-start.7 = (f32[4,12,32,128]{3,2,1,0:T(8,128)S(1)}, f32[4,12,32,128]{3,2,1,0:T(8,128)S(1)}, u32[]{:S(2)}, u32[]{:S(2)}) collective-permute-start(f32[4,12,32,128]{3,2,1,0:T(8,128)S(1)} %pad_maximum_fusion.pot), channel_id=1, source_target_pairs={{0,56},{32,8},{64,120},{96,72},{1,57},{33,9},{65,121},{97,73},{2,5... | collective-permute-start | bytes 2359304 | tf_op jit(solution)/shard_map/ppermute | solution.py:82
  28.2 19.9 %collective-permute-start.8 = (f32[4,12,32,128]{3,2,1,0:T(8,128)S(1)}, f32[4,12,32,128]{3,2,1,0:T(8,128)S(1)}, u32[]{:S(2)}, u32[]{:S(2)}) collective-permute-start(f32[4,12,32,128]{3,2,1,0:T(8,128)S(1)} %pad_maximum_fusion.pot), channel_id=1, source_target_pairs={{0,32},{32,0},{64,96},{96,64},{1,33},{33,1},{65,97},{97,65},{2,34}... | collective-permute-start | bytes 2359304 | tf_op jit(solution)/shard_map/ppermute | solution.py:82
  48.1 4.3 %collective-permute-start.9 = (f32[16,3,32,128]{3,2,1,0:T(8,128)S(1)}, f32[16,3,32,128]{3,2,1,0:T(8,128)S(1)}, u32[]{:S(2)}, u32[]{:S(2)}) collective-permute-start(f32[16,3,32,128]{3,2,1,0:T(8,128)S(1)} %all_to_all.5.own), channel_id=1, source_target_pairs={{0,32},{32,0},{64,96},{96,64},{1,33},{33,1},{65,97},{97,65},{2,34}... | collective-permute-start | bytes 2359304 | tf_op jit(solution)/shard_map/ppermute | solution.py:82
  50.3 2.2 %copy-start = (bf16[256,256]{1,0:T(8,128)(2,1)S(1)}, bf16[256,256]{1,0:T(8,128)(2,1)}, u32[]{:S(2)}) copy-start(bf16[256,256]{1,0:T(8,128)(2,1)} %constant.86.clone.zmat) | copy-start | bytes 393220
  50.3 2.2 %copy-start.1 = (bf16[32,224]{1,0:T(8,128)(2,1)S(1)}, bf16[32,224]{1,0:T(8,128)(2,1)}, u32[]{:S(2)}) copy-start(bf16[32,224]{1,0:T(8,128)(2,1)} %constant.87.clone.ymat) | copy-start | bytes 43012
  50.4 8.0 %collective-permute-start.10 = (f32[8,3,32,128]{3,2,1,0:T(8,128)S(1)}, f32[8,3,32,128]{3,2,1,0:T(8,128)S(1)}, u32[]{:S(2)}, u32[]{:S(2)}) collective-permute-start(f32[8,3,32,128]{3,2,1,0:T(8,128)S(1)} %pad_maximum_fusion.2), channel_id=1, source_target_pairs={{0,56},{32,8},{64,120},{96,72},{1,57},{33,9},{65,121},{97,73},{2,5... | collective-permute-start | bytes 1179656 | tf_op jit(solution)/shard_map/ppermute | solution.py:82
  51.6 10.6 %collective-permute-start.11 = (f32[8,3,32,128]{3,2,1,0:T(8,128)S(1)}, f32[8,3,32,128]{3,2,1,0:T(8,128)S(1)}, u32[]{:S(2)}, u32[]{:S(2)}) collective-permute-start(f32[8,3,32,128]{3,2,1,0:T(8,128)S(1)} %pad_maximum_fusion.3), channel_id=1, source_target_pairs={{0,56},{32,8},{64,120},{96,72},{1,57},{33,9},{65,121},{97,73},{2,5... | collective-permute-start | bytes 1179656 | tf_op jit(solution)/shard_map/ppermute | solution.py:82
  65.4 8.7 %collective-permute-start.12 = (f32[12,32,128]{2,1,0:T(8,128)S(1)}, f32[12,32,128]{2,1,0:T(8,128)S(1)}, u32[]{:S(2)}, u32[]{:S(2)}) collective-permute-start(f32[12,32,128]{2,1,0:T(8,128)S(1)} %get-tuple-element.34), channel_id=1, source_target_pairs={{0,64},{32,70},{64,0},{96,6},{1,65},{33,71},{65,1},{97,7},{2,66},{... | collective-permute-start | bytes 589832 | tf_op jit(solution)/shard_map/ppermute | solution.py:82
  67.4 8.8 %collective-permute-start.13 = (f32[12,32,128]{2,1,0:T(8,128)S(1)}, f32[12,32,128]{2,1,0:T(8,128)S(1)}, u32[]{:S(2)}, u32[]{:S(2)}) collective-permute-start(f32[12,32,128]{2,1,0:T(8,128)S(1)} %get-tuple-element.33), channel_id=1, source_target_pairs={{0,65},{32,71},{64,1},{96,7},{1,64},{33,70},{65,0},{97,6},{2,67},{... | collective-permute-start | bytes 589832 | tf_op jit(solution)/shard_map/ppermute | solution.py:82
  69.4 8.0 %collective-permute-start.14 = (f32[12,32,128]{2,1,0:T(8,128)S(1)}, f32[12,32,128]{2,1,0:T(8,128)S(1)}, u32[]{:S(2)}, u32[]{:S(2)}) collective-permute-start(f32[12,32,128]{2,1,0:T(8,128)S(1)} %get-tuple-element.32), channel_id=1, source_target_pairs={{0,66},{32,68},{64,2},{96,4},{1,67},{33,69},{65,3},{97,5},{2,64},{... | collective-permute-start | bytes 589832 | tf_op jit(solution)/shard_map/ppermute | solution.py:82
  70.2 11.4 %collective-permute-start.15 = (f32[12,32,128]{2,1,0:T(8,128)S(1)}, f32[12,32,128]{2,1,0:T(8,128)S(1)}, u32[]{:S(2)}, u32[]{:S(2)}) collective-permute-start(f32[12,32,128]{2,1,0:T(8,128)S(1)} %get-tuple-element.31), channel_id=1, source_target_pairs={{0,67},{32,69},{64,3},{96,5},{1,66},{33,68},{65,2},{97,4},{2,65},{... | collective-permute-start | bytes 589832 | tf_op jit(solution)/shard_map/ppermute | solution.py:82
  77.4 4.2 %copy-start.3 = (f32[4,12,32,128]{3,2,1,0:T(8,128)}, f32[4,12,32,128]{3,2,1,0:T(8,128)S(1)}, u32[]{:S(2)}) copy-start(f32[4,12,32,128]{3,2,1,0:T(8,128)S(1)} %bitcast_dynamic-update-slice_fusion.1) | copy-start | bytes 2359300

commit v4 on v3

--- a/solution.py
+++ b/solution.py
@@ -131,11 +131,11 @@
 
 
 def mix_kernel(rotation, first, second, third, out):
-    mix(rotation, ((0, first), (1, second), (2, third)), out, None)
+    mix(rotation, ((1, first), (3, second), (2, third)), out, None)
 
 
 def mix_last_kernel(rotation, fourth, sums, out):
-    mix(rotation, ((3, fourth),), out, sums)
+    mix(rotation, ((0, fourth),), out, sums)
 
 
 def block(a, b, w, w_at, zmat, ymat, at, first):
@@ -294,8 +294,8 @@
     next_z = permute(pair, lambda x, y, z, c: (x, y, 3 - z, c))
     pot = jnp.concatenate([pair, next_z])
     groups = [spread_run(part, r) for r, part in enumerate(cells)]
-    (sums,) = call(mix_kernel, [planes(16, RUN)], [], 3 << 20, rotation, *groups[:3], scalars=1)
-    (mixed,) = call(mix_last_kernel, [planes(16, RUN)], [], 1 << 20, rotation, groups[3], sums, scalars=1)
+    (sums,) = call(mix_kernel, [planes(16, RUN)], [], 3 << 20, rotation, groups[1], groups[3], groups[2], scalars=1)
+    (mixed,) = call(mix_last_kernel, [planes(16, RUN)], [], 1 << 20, rotation, groups[0], sums, scalars=1)
     pot_halo = permute(pot, x_neighbour)
     pot_other = permute(pot, other_core)
     plane_of_hosts = [[index_of(x, *chip, c) for chip in HOSTS] for x in range(4) for c in range(2)]

time: 82.5 us -> 82.2 us (level)
  starting transfers between devices: 35.4 us -> 37.3 us
  waiting for transfers between devices: 14.3 us -> 12.9 us
  blocking collectives: 15.3 us -> 14.4 us
    ppermute x16, starting transfers between devices: 35.4 us -> 37.3 us  [permute(): return lax.ppermute(array, AXES, pairs)]
    ppermute x16, waiting for transfers between devices: 14.3 us -> 12.9 us  [permute(): return lax.ppermute(array, AXES, pairs)]
    all_to_all x1, blocking collectives: 15.3 us -> 14.4 us  [local(): lax.all_to_all(mixed, AXES, 0, 0, tiled=True, axis_index_groups=plane_of_...]
  transfers between devices with their start and end apart: 16 -> 16, of which waited for: 8 -> 7; matrix products, arithmetic and copies ran while one was open for 2% -> 2% of each run, Pallas kernels for 14% -> 14%
where the time goes in v4:
time: 82.2 us; the launch traced here: 81.9 us
  starting transfers between devices  37.3 us (45%)
  Pallas kernels  14.7 us (18%)
  blocking collectives  14.4 us (18%)
  waiting for transfers between devices  12.9 us (16%)
  local copies, waits for them, and re-layouts  2.23 us (3%)
    ppermute x16, starting transfers between devices, permute(): return lax.ppermute(array, AXES, pairs)  37.3 us
    pallas_call x5, Pallas kernels, call(): pl.pallas_call(kernel, out_shape=outs, in_specs=specs, out_specs=vmem(len...  14.7 us
    all_to_all x1, blocking collectives, local(): lax.all_to_all(mixed, AXES, 0, 0, tiled=True, axis_index_groups=plane_of_...  14.4 us
    ppermute x16, waiting for transfers between devices, permute(): return lax.ppermute(array, AXES, pairs)  12.9 us
  transfers between devices with their start and end apart: 16, of which 7 were waited for; matrix products, arithmetic and copies ran while one was open for 2% of the time, Pallas kernels for 14%

profile of v4, /device:TPU:1, one launch (start us, length us, event | category | flops | bytes accessed | tf_op | source)
XLA Modules:
  0.0 81.9 jit_solution(13427864928106355453)
XLA Ops:
  0.0 1.4 %collective-permute-start = (f32[12,32,128]{2,1,0:T(8,128)}, f32[12,32,128]{2,1,0:T(8,128)S(1)}, u32[]{:S(2)}, u32[]{:S(2)}) collective-permute-start(f32[12,32,128]{2,1,0:T(8,128)} %param.6), channel_id=1, source_target_pairs={{0,6},{64,70},{1,7},{65,71},{2,4},{66,68},{3,5},{67,69},{36,34},{1... | collective-permute-start | bytes 589832 | tf_op jit(solution)/shard_map/ppermute | solution.py:82
  1.4 4.4 %collective-permute-start.5 = (f32[12,32,128]{2,1,0:T(8,128)}, f32[12,32,128]{2,1,0:T(8,128)S(1)}, u32[]{:S(2)}, u32[]{:S(2)}) collective-permute-start(f32[12,32,128]{2,1,0:T(8,128)} %param.6), channel_id=1, source_target_pairs={{0,2},{32,4},{64,66},{96,68},{1,3},{33,5},{65,67},{97,69},{2,0},{3... | collective-permute-start | bytes 589832 | tf_op jit(solution)/shard_map/ppermute | solution.py:82
  5.8 1.3 %constant_dynamic-slice_fusion = (f32[4,3,32,128]{3,2,1,0:T(8,128)S(1)}, f32[4,3,32,128]{3,2,1,0:T(8,128)S(1)}, f32[4,3,32,128]{3,2,1,0:T(8,128)S(1)}, f32[4,3,32,128]{3,2,1,0:T(8,128)S(1)}) fusion(f32[4,12,32,128]{3,2,1,0:T(8,128)} %param.5, s32[]{:T(128)S(6)} %select_n.74, s32[]{:T(128)S(6)} %select_n.72, s32[]{:T(128)S(6)} %select_n.71, s32[]{:T(128)S(6)} %select_n.73), kind=kLoop, calls=%fused_computation.13 | loop fusion | bytes 1572880 | tf_op jit(solution)/shard_map/dynamic_slice | solution.py:288
  7.1 2.3 %collective-permute-done = f32[12,32,128]{2,1,0:T(8,128)S(1)} collective-permute-done((f32[12,32,128]{2,1,0:T(8,128)}, f32[12,32,128]{2,1,0:T(8,128)S(1)}, u32[]{:S(2)}, u32[]{:S(2)}) %collective-permute-start) | collective-permute-done | bytes 196640 | tf_op jit(solution)/shard_map/ppermute | solution.py:82
  9.4 1.9 %collective-permute-done.5 = f32[12,32,128]{2,1,0:T(8,128)S(1)} collective-permute-done((f32[12,32,128]{2,1,0:T(8,128)}, f32[12,32,128]{2,1,0:T(8,128)S(1)}, u32[]{:S(2)}, u32[]{:S(2)}) %collective-permute-start.5) | collective-permute-done | bytes 196640 | tf_op jit(solution)/shard_map/ppermute | solution.py:82
  11.4 3.5 %collective-permute-start.6 = (f32[2,12,32,128]{3,2,1,0:T(8,128)S(1)}, f32[2,12,32,128]{3,2,1,0:T(8,128)S(1)}, u32[]{:S(2)}, u32[]{:S(2)}) collective-permute-start(f32[2,12,32,128]{3,2,1,0:T(8,128)S(1)} %pad_maximum_fusion.1), channel_id=1, source_target_pairs={{0,65},{32,97},{64,1},{96,33},{1,64},{33,96},{65,0},{97,32},{2,67}... | collective-permute-start | bytes 1179656 | tf_op jit(solution)/shard_map/ppermute | solution.py:82
  14.8 3.2 %collective-permute-start.2 = (f32[4,3,32,128]{3,2,1,0:T(8,128)S(1)}, f32[4,3,32,128]{3,2,1,0:T(8,128)S(1)}, u32[]{:S(2)}, u32[]{:S(2)}) collective-permute-start(f32[4,3,32,128]{3,2,1,0:T(8,128)S(1)} %get-tuple-element.19), channel_id=1, source_target_pairs={{0,64},{32,70},{64,0},{96,6},{1,65},{33,71},{65,1},{97,7},{2,66},{... | collective-permute-start | bytes 589832 | tf_op jit(solution)/shard_map/ppermute | solution.py:82
  18.3 2.0 %collective-permute-start.4 = (f32[4,3,32,128]{3,2,1,0:T(8,128)S(1)}, f32[4,3,32,128]{3,2,1,0:T(8,128)S(1)}, u32[]{:S(2)}, u32[]{:S(2)}) collective-permute-start(f32[4,3,32,128]{3,2,1,0:T(8,128)S(1)} %get-tuple-element.21), channel_id=1, source_target_pairs={{0,6},{32,0},{64,70},{96,64},{1,7},{33,1},{65,71},{97,65},{2,4},{3... | collective-permute-start | bytes 589832 | tf_op jit(solution)/shard_map/ppermute | solution.py:82
  20.3 6.1 %collective-permute-start.1 = (f32[4,3,32,128]{3,2,1,0:T(8,128)S(1)}, f32[4,3,32,128]{3,2,1,0:T(8,128)S(1)}, u32[]{:S(2)}, u32[]{:S(2)}) collective-permute-start(f32[4,3,32,128]{3,2,1,0:T(8,128)S(1)} %get-tuple-element.18), channel_id=1, source_target_pairs={{0,0},{32,6},{64,64},{96,70},{1,1},{33,7},{65,65},{97,71},{2,2},{3... | collective-permute-start | bytes 589832 | tf_op jit(solution)/shard_map/ppermute | solution.py:82
  26.8 2.6 %collective-permute-start.8 = (f32[4,12,32,128]{3,2,1,0:T(8,128)S(1)}, f32[4,12,32,128]{3,2,1,0:T(8,128)S(1)}, u32[]{:S(2)}, u32[]{:S(2)}) collective-permute-start(f32[4,12,32,128]{3,2,1,0:T(8,128)S(1)} %pad_maximum_fusion.pot), channel_id=1, source_target_pairs={{0,32},{32,0},{64,96},{96,64},{1,33},{33,1},{65,97},{97,65},{2,34}... | collective-permute-start | bytes 2359304 | tf_op jit(solution)/shard_map/ppermute | solution.py:82
  29.5 1.0 %collective-permute-done.4.third = f32[4,3,32,128]{3,2,1,0:T(8,128)S(1)} collective-permute-done((f32[4,3,32,128]{3,2,1,0:T(8,128)S(1)}, f32[4,3,32,128]{3,2,1,0:T(8,128)S(1)}, u32[]{:S(2)}, u32[]{:S(2)}) %collective-permute-start.4) | collective-permute-done | bytes 196640 | tf_op jit(solution)/shard_map/ppermute | solution.py:82
  30.5 1.4 %shard_map.55.sums = f32[16,3,32,128]{3,2,1,0:T(8,128)S(1)} custom-call(f32[16,16]{1,0:T(8,128)S(1)} %copy-done.2, f32[4,3,32,128]{3,2,1,0:T(8,128)S(1)} %collective-permute-done.2.first, f32[4,3,32,128]{3,2,1,0:T(8,128)S(1)} %collective-permute-done.3.second, f32[4,3,32,128]{3,2,1,0:T(8,128)S(1)} %collective-permute-done.4.third), custom_call_target="tpu_custom_call" | custom-call | flops 3145728 | bytes 1377280 | tf_op jit(solution)/shard_map/pallas_call | solution.py:266
  32.8 14.4 %all_to_all.5.own = f32[16,3,32,128]{3,2,1,0:T(8,128)S(1)} all-to-all(f32[16,3,32,128]{3,2,1,0:T(8,128)S(1)} %shard_map.56), channel_id=1, replica_groups={{64,65,66,67,68,69,70,71,0,1,2,3,4,5,6,7},{96,97,98,99,100,101,102,103,..., dimensions={0} | all-to-all | bytes 1572864 | tf_op jit(solution)/shard_map/all_to_all | solution.py:302
  47.2 2.7 %collective-permute-start.9 = (f32[16,3,32,128]{3,2,1,0:T(8,128)S(1)}, f32[16,3,32,128]{3,2,1,0:T(8,128)S(1)}, u32[]{:S(2)}, u32[]{:S(2)}) collective-permute-start(f32[16,3,32,128]{3,2,1,0:T(8,128)S(1)} %all_to_all.5.own), channel_id=1, source_target_pairs={{0,32},{32,0},{64,96},{96,64},{1,33},{33,1},{65,97},{97,65},{2,34}... | collective-permute-start | bytes 2359304 | tf_op jit(solution)/shard_map/ppermute | solution.py:82
  50.9 1.2 %collective-permute-start.11 = (f32[8,3,32,128]{3,2,1,0:T(8,128)S(1)}, f32[8,3,32,128]{3,2,1,0:T(8,128)S(1)}, u32[]{:S(2)}, u32[]{:S(2)}) collective-permute-start(f32[8,3,32,128]{3,2,1,0:T(8,128)S(1)} %pad_maximum_fusion.3), channel_id=1, source_target_pairs={{0,56},{32,8},{64,120},{96,72},{1,57},{33,9},{65,121},{97,73},{2,5... | collective-permute-start | bytes 1179656 | tf_op jit(solution)/shard_map/ppermute | solution.py:82
  52.1 5.9 %shard_map.57 = (f32[54,32,128]{2,1,0:T(8,128)S(1)}, f32[54,32,128]{2,1,0:T(8,128)S(1)}, f32[48,32,128]{2,1,0:T(8,128)S(1)}) custom-call(f32[16,3,32,128]{3,2,1,0:T(8,128)S(1)} %all_to_all.5.own, f32[16,3,32,128]{3,2,1,0:T(8,128)S(1)} %collective-permute-done.9.other, f32[4,12,32,128]{3,2,1,0:T(8,128)S(1)} %pad_maximum_fusion.pot, ...), custom_call_target="tpu_custom_call" | custom-call | flops 536870912 | bytes 5992448 | tf_op jit(solution)/shard_map/pallas_call | solution.py:266
  58.0 3.3 %shard_map.58 = (f32[72,32,128]{2,1,0:T(8,128)S(1)}, f32[72,32,128]{2,1,0:T(8,128)S(1)}) custom-call(f32[54,32,128]{2,1,0:T(8,128)S(1)} %get-tuple-element.25.even_in, f32[54,32,128]{2,1,0:T(8,128)S(1)} %get-tuple-element.26.odd_in, f32[48,32,128]{2,1,0:T(8,128)S(1)} %get-tuple-element.27.w_in, f32[8,3,32,128]{3,2,1,0:T(8,128)S(1)} %collective-permute-done.10.halo, ...), custom_call_target="tpu_custom_call" | custom-call | flops 268435456 | bytes 6385664 | tf_op jit(solution)/shard_map/pallas_call | solution.py:266
  61.8 3.2 %shard_map.59 = f32[4,12,32,128]{3,2,1,0:T(8,128)S(1)} custom-call(f32[72,32,128]{2,1,0:T(8,128)S(1)} %get-tuple-element.29.even_in, f32[72,32,128]{2,1,0:T(8,128)S(1)} %get-tuple-element.30.odd_in, f32[48,32,128]{2,1,0:T(8,128)S(1)} %get-tuple-element.27.w_in, f32[8,3,32,128]{3,2,1,0:T(8,128)S(1)} %collective-permute-done.11.halo, ...), custom_call_target="tpu_custom_call" | custom-call | flops 268435456 | bytes 5402624 | tf_op jit(solution)/shard_map/pallas_call | solution.py:266
  65.1 2.1 %collective-permute-start.12 = (f32[12,32,128]{2,1,0:T(8,128)S(1)}, f32[12,32,128]{2,1,0:T(8,128)S(1)}, u32[]{:S(2)}, u32[]{:S(2)}) collective-permute-start(f32[12,32,128]{2,1,0:T(8,128)S(1)} %get-tuple-element.34), channel_id=1, source_target_pairs={{0,64},{32,70},{64,0},{96,6},{1,65},{33,71},{65,1},{97,7},{2,66},{... | collective-permute-start | bytes 589832 | tf_op jit(solution)/shard_map/ppermute | solution.py:82
  67.1 1.9 %collective-permute-start.13 = (f32[12,32,128]{2,1,0:T(8,128)S(1)}, f32[12,32,128]{2,1,0:T(8,128)S(1)}, u32[]{:S(2)}, u32[]{:S(2)}) collective-permute-start(f32[12,32,128]{2,1,0:T(8,128)S(1)} %get-tuple-element.33), channel_id=1, source_target_pairs={{0,65},{32,71},{64,1},{96,7},{1,64},{33,70},{65,0},{97,6},{2,67},{... | collective-permute-start | bytes 589832 | tf_op jit(solution)/shard_map/ppermute | solution.py:82
  69.1 1.0 %collective-permute-start.14 = (f32[12,32,128]{2,1,0:T(8,128)S(1)}, f32[12,32,128]{2,1,0:T(8,128)S(1)}, u32[]{:S(2)}, u32[]{:S(2)}) collective-permute-start(f32[12,32,128]{2,1,0:T(8,128)S(1)} %get-tuple-element.32), channel_id=1, source_target_pairs={{0,66},{32,68},{64,2},{96,4},{1,67},{33,69},{65,3},{97,5},{2,64},{... | collective-permute-start | bytes 589832 | tf_op jit(solution)/shard_map/ppermute | solution.py:82
  70.1 3.7 %collective-permute-start.15 = (f32[12,32,128]{2,1,0:T(8,128)S(1)}, f32[12,32,128]{2,1,0:T(8,128)S(1)}, u32[]{:S(2)}, u32[]{:S(2)}) collective-permute-start(f32[12,32,128]{2,1,0:T(8,128)S(1)} %get-tuple-element.31), channel_id=1, source_target_pairs={{0,67},{32,69},{64,3},{96,5},{1,66},{33,68},{65,2},{97,4},{2,65},{... | collective-permute-start | bytes 589832 | tf_op jit(solution)/shard_map/ppermute | solution.py:82
  73.9 2.2 %collective-permute-done.13 = f32[12,32,128]{2,1,0:T(8,128)S(1)} collective-permute-done((f32[12,32,128]{2,1,0:T(8,128)S(1)}, f32[12,32,128]{2,1,0:T(8,128)S(1)}, u32[]{:S(2)}, u32[]{:S(2)}) %collective-permute-start.13) | collective-permute-done | bytes 196640 | tf_op jit(solution)/shard_map/ppermute | solution.py:82
  77.1 4.2 %collective-permute-done.15 = f32[12,32,128]{2,1,0:T(8,128)S(1)} collective-permute-done((f32[12,32,128]{2,1,0:T(8,128)S(1)}, f32[12,32,128]{2,1,0:T(8,128)S(1)}, u32[]{:S(2)}, u32[]{:S(2)}) %collective-permute-start.15) | collective-permute-done | bytes 196640 | tf_op jit(solution)/shard_map/ppermute | solution.py:82
  (38 shorter events, 4.9 us)
Async XLA Ops:
  0.0 9.3 %copy-start.4 = (f32[12,32,128]{2,1,0:T(8,128)S(1)}, f32[12,32,128]{2,1,0:T(8,128)}, u32[]{:S(2)}) copy-start(f32[12,32,128]{2,1,0:T(8,128)} %param.6) | copy-start | bytes 589828
  0.0 9.3 %collective-permute-start = (f32[12,32,128]{2,1,0:T(8,128)}, f32[12,32,128]{2,1,0:T(8,128)S(1)}, u32[]{:S(2)}, u32[]{:S(2)}) collective-permute-start(f32[12,32,128]{2,1,0:T(8,128)} %param.6), channel_id=1, source_target_pairs={{0,6},{64,70},{1,7},{65,71},{2,4},{66,68},{3,5},{67,69},{36,34},{1... | collective-permute-start | bytes 589832 | tf_op jit(solution)/shard_map/ppermute | solution.py:82
  1.4 9.9 %collective-permute-start.5 = (f32[12,32,128]{2,1,0:T(8,128)}, f32[12,32,128]{2,1,0:T(8,128)S(1)}, u32[]{:S(2)}, u32[]{:S(2)}) collective-permute-start(f32[12,32,128]{2,1,0:T(8,128)} %param.6), channel_id=1, source_target_pairs={{0,2},{32,4},{64,66},{96,68},{1,3},{33,5},{65,67},{97,69},{2,0},{3... | collective-permute-start | bytes 589832 | tf_op jit(solution)/shard_map/ppermute | solution.py:82
  11.3 19.1 %copy-start.2 = (f32[16,16]{1,0:T(8,128)S(1)}, f32[16,16]{1,0:T(8,128)}, u32[]{:S(2)}) copy-start(f32[16,16]{1,0:T(8,128)} %rotation.3) | copy-start | bytes 3076
  11.4 15.1 %collective-permute-start.6 = (f32[2,12,32,128]{3,2,1,0:T(8,128)S(1)}, f32[2,12,32,128]{3,2,1,0:T(8,128)S(1)}, u32[]{:S(2)}, u32[]{:S(2)}) collective-permute-start(f32[2,12,32,128]{3,2,1,0:T(8,128)S(1)} %pad_maximum_fusion.1), channel_id=1, source_target_pairs={{0,65},{32,97},{64,1},{96,33},{1,64},{33,96},{65,0},{97,32},{2,67}... | collective-permute-start | bytes 1179656 | tf_op jit(solution)/shard_map/ppermute | solution.py:82
  14.8 12.0 %collective-permute-start.2 = (f32[4,3,32,128]{3,2,1,0:T(8,128)S(1)}, f32[4,3,32,128]{3,2,1,0:T(8,128)S(1)}, u32[]{:S(2)}, u32[]{:S(2)}) collective-permute-start(f32[4,3,32,128]{3,2,1,0:T(8,128)S(1)} %get-tuple-element.19), channel_id=1, source_target_pairs={{0,64},{32,70},{64,0},{96,6},{1,65},{33,71},{65,1},{97,7},{2,66},{... | collective-permute-start | bytes 589832 | tf_op jit(solution)/shard_map/ppermute | solution.py:82
  18.0 11.5 %collective-permute-start.3 = (f32[4,3,32,128]{3,2,1,0:T(8,128)S(1)}, f32[4,3,32,128]{3,2,1,0:T(8,128)S(1)}, u32[]{:S(2)}, u32[]{:S(2)}) collective-permute-start(f32[4,3,32,128]{3,2,1,0:T(8,128)S(1)} %get-tuple-element.20), channel_id=1, source_target_pairs={{0,70},{32,64},{64,6},{96,0},{1,71},{33,65},{65,7},{97,1},{2,68},{... | collective-permute-start | bytes 589832 | tf_op jit(solution)/shard_map/ppermute | solution.py:82
  18.3 12.2 %collective-permute-start.4 = (f32[4,3,32,128]{3,2,1,0:T(8,128)S(1)}, f32[4,3,32,128]{3,2,1,0:T(8,128)S(1)}, u32[]{:S(2)}, u32[]{:S(2)}) collective-permute-start(f32[4,3,32,128]{3,2,1,0:T(8,128)S(1)} %get-tuple-element.21), channel_id=1, source_target_pairs={{0,6},{32,0},{64,70},{96,64},{1,7},{33,1},{65,71},{97,65},{2,4},{3... | collective-permute-start | bytes 589832 | tf_op jit(solution)/shard_map/ppermute | solution.py:82
  20.3 11.5 %collective-permute-start.1 = (f32[4,3,32,128]{3,2,1,0:T(8,128)S(1)}, f32[4,3,32,128]{3,2,1,0:T(8,128)S(1)}, u32[]{:S(2)}, u32[]{:S(2)}) collective-permute-start(f32[4,3,32,128]{3,2,1,0:T(8,128)S(1)} %get-tuple-element.18), channel_id=1, source_target_pairs={{0,0},{32,6},{64,64},{96,70},{1,1},{33,7},{65,65},{97,71},{2,2},{3... | collective-permute-start | bytes 589832 | tf_op jit(solution)/shard_map/ppermute | solution.py:82
  26.5 20.7 %collective-permute-start.7 = (f32[4,12,32,128]{3,2,1,0:T(8,128)S(1)}, f32[4,12,32,128]{3,2,1,0:T(8,128)S(1)}, u32[]{:S(2)}, u32[]{:S(2)}) collective-permute-start(f32[4,12,32,128]{3,2,1,0:T(8,128)S(1)} %pad_maximum_fusion.pot), channel_id=1, source_target_pairs={{0,56},{32,8},{64,120},{96,72},{1,57},{33,9},{65,121},{97,73},{2,5... | collective-permute-start | bytes 2359304 | tf_op jit(solution)/shard_map/ppermute | solution.py:82
  26.8 20.4 %collective-permute-start.8 = (f32[4,12,32,128]{3,2,1,0:T(8,128)S(1)}, f32[4,12,32,128]{3,2,1,0:T(8,128)S(1)}, u32[]{:S(2)}, u32[]{:S(2)}) collective-permute-start(f32[4,12,32,128]{3,2,1,0:T(8,128)S(1)} %pad_maximum_fusion.pot), channel_id=1, source_target_pairs={{0,32},{32,0},{64,96},{96,64},{1,33},{33,1},{65,97},{97,65},{2,34}... | collective-permute-start | bytes 2359304 | tf_op jit(solution)/shard_map/ppermute | solution.py:82
  47.2 4.9 %collective-permute-start.9 = (f32[16,3,32,128]{3,2,1,0:T(8,128)S(1)}, f32[16,3,32,128]{3,2,1,0:T(8,128)S(1)}, u32[]{:S(2)}, u32[]{:S(2)}) collective-permute-start(f32[16,3,32,128]{3,2,1,0:T(8,128)S(1)} %all_to_all.5.own), channel_id=1, source_target_pairs={{0,32},{32,0},{64,96},{96,64},{1,33},{33,1},{65,97},{97,65},{2,34}... | collective-permute-start | bytes 2359304 | tf_op jit(solution)/shard_map/ppermute | solution.py:82
  49.9 2.2 %copy-start = (bf16[256,256]{1,0:T(8,128)(2,1)S(1)}, bf16[256,256]{1,0:T(8,128)(2,1)}, u32[]{:S(2)}) copy-start(bf16[256,256]{1,0:T(8,128)(2,1)} %constant.86.clone.zmat) | copy-start | bytes 393220
  49.9 2.2 %copy-start.1 = (bf16[32,224]{1,0:T(8,128)(2,1)S(1)}, bf16[32,224]{1,0:T(8,128)(2,1)}, u32[]{:S(2)}) copy-start(bf16[32,224]{1,0:T(8,128)(2,1)} %constant.87.clone.ymat) | copy-start | bytes 43012
  50.0 8.0 %collective-permute-start.10 = (f32[8,3,32,128]{3,2,1,0:T(8,128)S(1)}, f32[8,3,32,128]{3,2,1,0:T(8,128)S(1)}, u32[]{:S(2)}, u32[]{:S(2)}) collective-permute-start(f32[8,3,32,128]{3,2,1,0:T(8,128)S(1)} %pad_maximum_fusion.2), channel_id=1, source_target_pairs={{0,56},{32,8},{64,120},{96,72},{1,57},{33,9},{65,121},{97,73},{2,5... | collective-permute-start | bytes 1179656 | tf_op jit(solution)/shard_map/ppermute | solution.py:82
  50.9 10.9 %collective-permute-start.11 = (f32[8,3,32,128]{3,2,1,0:T(8,128)S(1)}, f32[8,3,32,128]{3,2,1,0:T(8,128)S(1)}, u32[]{:S(2)}, u32[]{:S(2)}) collective-permute-start(f32[8,3,32,128]{3,2,1,0:T(8,128)S(1)} %pad_maximum_fusion.3), channel_id=1, source_target_pairs={{0,56},{32,8},{64,120},{96,72},{1,57},{33,9},{65,121},{97,73},{2,5... | collective-permute-start | bytes 1179656 | tf_op jit(solution)/shard_map/ppermute | solution.py:82
  65.1 8.7 %collective-permute-start.12 = (f32[12,32,128]{2,1,0:T(8,128)S(1)}, f32[12,32,128]{2,1,0:T(8,128)S(1)}, u32[]{:S(2)}, u32[]{:S(2)}) collective-permute-start(f32[12,32,128]{2,1,0:T(8,128)S(1)} %get-tuple-element.34), channel_id=1, source_target_pairs={{0,64},{32,70},{64,0},{96,6},{1,65},{33,71},{65,1},{97,7},{2,66},{... | collective-permute-start | bytes 589832 | tf_op jit(solution)/shard_map/ppermute | solution.py:82
  67.1 8.9 %collective-permute-start.13 = (f32[12,32,128]{2,1,0:T(8,128)S(1)}, f32[12,32,128]{2,1,0:T(8,128)S(1)}, u32[]{:S(2)}, u32[]{:S(2)}) collective-permute-start(f32[12,32,128]{2,1,0:T(8,128)S(1)} %get-tuple-element.33), channel_id=1, source_target_pairs={{0,65},{32,71},{64,1},{96,7},{1,64},{33,70},{65,0},{97,6},{2,67},{... | collective-permute-start | bytes 589832 | tf_op jit(solution)/shard_map/ppermute | solution.py:82
  69.1 7.9 %collective-permute-start.14 = (f32[12,32,128]{2,1,0:T(8,128)S(1)}, f32[12,32,128]{2,1,0:T(8,128)S(1)}, u32[]{:S(2)}, u32[]{:S(2)}) collective-permute-start(f32[12,32,128]{2,1,0:T(8,128)S(1)} %get-tuple-element.32), channel_id=1, source_target_pairs={{0,66},{32,68},{64,2},{96,4},{1,67},{33,69},{65,3},{97,5},{2,64},{... | collective-permute-start | bytes 589832 | tf_op jit(solution)/shard_map/ppermute | solution.py:82
  70.1 11.2 %collective-permute-start.15 = (f32[12,32,128]{2,1,0:T(8,128)S(1)}, f32[12,32,128]{2,1,0:T(8,128)S(1)}, u32[]{:S(2)}, u32[]{:S(2)}) collective-permute-start(f32[12,32,128]{2,1,0:T(8,128)S(1)} %get-tuple-element.31), channel_id=1, source_target_pairs={{0,67},{32,69},{64,3},{96,5},{1,66},{33,68},{65,2},{97,4},{2,65},{... | collective-permute-start | bytes 589832 | tf_op jit(solution)/shard_map/ppermute | solution.py:82
  77.0 4.2 %copy-start.3 = (f32[4,12,32,128]{3,2,1,0:T(8,128)}, f32[4,12,32,128]{3,2,1,0:T(8,128)S(1)}, u32[]{:S(2)}) copy-start(f32[4,12,32,128]{3,2,1,0:T(8,128)S(1)} %bitcast_dynamic-update-slice_fusion.1) | copy-start | bytes 2359300
